TPU v7x, 128 devices: a whole 4x4x4 slice. The times are simulated.
128 devices in a mesh: client: 4 (over x), row: 4 (over z_lo, core), col: 8 (over y, z_hi).
Axes of the slice: x: 4, y: 4, z: 4 (z_hi: 2, z_lo: 2; z = z_hi * 2 + z_lo), core: 2. Of those that a mesh axis runs over, the one named last changes fastest.
Arguments:
- frozen_up_weight: bfloat16 [2, 8192, 28672], P(None, 'client', ('row', 'col')), may hold values from -3 to 3
- adapter_down_stack: bfloat16 [2, 256, 8192], P(None, ('row', 'col'), 'client'), may hold values from -6 to 6
- adapter_up_stack: bfloat16 [2, 256, 28672], P(None, 'client', ('row', 'col')), may hold values from -0.375 to 0.375
- participant_weight: float32 [16], replicated, may hold values from 0.25 to 1
Outputs:
- merged: bfloat16 [2, 8192, 28672], P(None, ('client', 'row', 'col'))
All inputs are finite; a program needn't handle non-finite values.
Results may differ from a plain program's by a relative error of at most 0.0042.
Values may be sent and summed in bfloat16 or wider, within the bound.
No kernel may reach another device: no remote copies, remote signals or barrier semaphores. Data moves between devices by JAX's collectives and lax.ppermute only.
A program may use at most 128 MiB of HBM per device.

v0:
```python
import jax
import jax.numpy as jnp
from jax import lax
from jax.sharding import PartitionSpec as P

RANK = 16
CLIENTS = 16


def scale_ranks(piece, participant_weight):
    ranks = jnp.arange(piece.shape[0], dtype=jnp.int32)
    owners = ranks // RANK
    table = jnp.arange(CLIENTS, dtype=jnp.int32)
    weights = jnp.sum(
        jnp.where(owners[:, None] == table[None, :], participant_weight[None, :], 0.0), axis=1
    )
    return (weights[:, None] * piece.astype(jnp.float32)).astype(jnp.bfloat16)


def contract_ranks(left, right):
    return lax.dot_general(
        left, right, (((0,), (0,)), ((), ())), preferred_element_type=jnp.float32
    )


def local(frozen_up_weight, adapter_down_stack, adapter_up_stack, participant_weight):
    results = []
    for layer_index in range(frozen_up_weight.shape[0]):
        base_tile = frozen_up_weight[layer_index]
        down_factor_slice = adapter_down_stack[layer_index]
        up_factor_slice = adapter_up_stack[layer_index]
        b_stacked = lax.all_gather(up_factor_slice, "client", axis=0, tiled=True)
        base_rows = lax.all_to_all(
            base_tile, ("row", "col"), split_axis=0, concat_axis=1, tiled=True
        )
        a_rows = lax.all_to_all(
            down_factor_slice, ("row", "col"), split_axis=1, concat_axis=0, tiled=True
        )
        scaled_update = scale_ranks(a_rows, participant_weight)
        delta = contract_ranks(
            scaled_update, lax.all_gather(b_stacked, ("row", "col"), axis=1, tiled=True)
        )
        owned = (base_rows.astype(jnp.float32) + delta).astype(jnp.bfloat16)
        results.append(owned)
    return jnp.stack(results)


def solution(mesh):
    return jax.shard_map(
        local,
        mesh=mesh,
        in_specs=(
            P(None, "client", ("row", "col")),
            P(None, ("row", "col"), "client"),
            P(None, "client", ("row", "col")),
            P(),
        ),
        out_specs=P(None, ("client", "row", "col"), None),
        check_vma=False,
    )
```

profile of v0, /device:TPU:1, one launch (start us, length us, event | category | flops | bytes accessed | tf_op | source)
XLA Modules:
  0.0 330.7 jit_solution(13855406793108093656)
XLA Ops:
  6.5 0.0 all-gather.9.cloned.1.call-start
  6.5 1.0 fusion.13
  7.5 12.5 %all-gather.2 = bf16[1,256,896]{2,1,0:T(8,128)(2,1)} all-gather(bf16[1,64,896]{2,1,0:T(8,128)(2,1)S(1)} %get-tuple-element.8), channel_id=4, replica_groups=mesh['client'=4,'row'=4,'col'=8] {'client'}, dimensions={1}, use_global_device_ids=true | all-gather | bytes 573440 | tf_op jit(solution)/shard_map/all_gather | solution.py:32
  20.1 0.0 all-gather.9.cloned.1.call-update
  20.1 0.0 all-gather.7.cloned.1.call-start
  20.1 10.5 %all-gather = bf16[1,256,896]{2,1,0:T(8,128)(2,1)} all-gather(bf16[1,64,896]{2,1,0:T(8,128)(2,1)S(1)} %get-tuple-element.7), channel_id=2, replica_groups=mesh['client'=4,'row'=4,'col'=8] {'client'}, dimensions={1}, use_global_device_ids=true | all-gather | bytes 573440 | tf_op jit(solution)/shard_map/all_gather | solution.py:32
  30.6 0.0 all-gather.7.cloned.1.call-update
  30.7 0.8 fusion.14
  31.4 0.1 all_to_all.46
  31.6 0.7 reshape.47
  32.3 13.8 %all-to-all-start.3 = ((bf16[32,2,256]{2,1,0:T(2,128)(2,1)}), bf16[32,2,256]{2,1,0:T(2,128)(2,1)S(1)}, u32[]{:S(2)}, u32[]{:S(2)}) async-start(bf16[32,2,256]{2,1,0:T(2,128)(2,1)} %reshape.47), calls=%async_computation.3 | async-start | bytes 65536 | tf_op jit(solution)/shard_map/all_to_all | solution.py:36
  46.2 0.1 all_to_all.42
  46.3 0.7 reshape.49
  47.1 6.3 %all-to-all-done.3 = bf16[32,2,256]{2,1,0:T(2,128)(2,1)S(1)} async-done(((bf16[32,2,256]{2,1,0:T(2,128)(2,1)}), bf16[32,2,256]{2,1,0:T(2,128)(2,1)S(1)}, u32[]{:S(2)}, u32[]{:S(2)}) %all-to-all-start.3) | async-done | bytes 32800 | tf_op jit(solution)/shard_map/all_to_all | solution.py:36
  53.4 3.9 %all-to-all-start.1 = ((bf16[32,2,256]{2,1,0:T(2,128)(2,1)}), bf16[32,2,256]{2,1,0:T(2,128)(2,1)S(1)}, u32[]{:S(2)}, u32[]{:S(2)}) async-start(bf16[32,2,256]{2,1,0:T(2,128)(2,1)} %reshape.49), calls=%async_computation.1 | async-start | bytes 65536 | tf_op jit(solution)/shard_map/all_to_all | solution.py:36
  57.3 6.9 %fusion.12 = (bf16[1,2048,896]{2,1,0:T(8,128)(2,1)}, bf16[1,2048,896]{2,1,0:T(8,128)(2,1)}) fusion(bf16[2,2048,896]{2,1,0:T(8,128)(2,1)} %param.4), kind=kLoop, calls=%fused_computation.23 | loop fusion | bytes 14680064 | tf_op jit(solution)/shard_map/slice | solution.py:29
  64.3 0.3 all-to-all-done.1
  64.5 0.0 copy-start.1
  64.5 67.1 %all_to_all.52 = bf16[32,64,896]{2,1,0:T(8,128)(2,1)} all-to-all(bf16[32,64,896]{2,1,0:T(8,128)(2,1)} %bitcast.53), channel_id=1, replica_groups=mesh['client'=4,'row'=4,'col'=8] {'row','col'}, dimensions={0} | all-to-all | bytes 7340032 | tf_op jit(solution)/shard_map/all_to_all | solution.py:33
  131.6 4.6 %all-to-all-start = ((bf16[32,64,896]{2,1,0:T(8,128)(2,1)}), bf16[32,64,896]{2,1,0:T(8,128)(2,1)}, u32[]{:S(2)}, u32[]{:S(2)}) async-start(bf16[32,64,896]{2,1,0:T(8,128)(2,1)} %bitcast.52), calls=%async_computation | async-start | bytes 7340032 | tf_op jit(solution)/shard_map/all_to_all | solution.py:33
  136.3 0.0 copy-done.1
  136.3 0.1 select_reduce_fusion
  136.4 0.1 reshape.48
  136.5 0.1 reshape.50
  136.6 3.0 convert_bitcast_fusion
  139.6 3.5 %copy.20 = f32[32,8,8,896]{3,2,0,1:T(8,128)} copy(f32[32,8,8,896]{3,2,1,0:T(8,128)S(1)} %convert_bitcast_fusion) | data formatting | bytes 14680064 | tf_op jit(solution)/shard_map/convert_element_type | solution.py:43
  143.1 52.2 %all-to-all-done = bf16[32,64,896]{2,1,0:T(8,128)(2,1)} async-done(((bf16[32,64,896]{2,1,0:T(8,128)(2,1)}), bf16[32,64,896]{2,1,0:T(8,128)(2,1)}, u32[]{:S(2)}, u32[]{:S(2)}) %all-to-all-start) | async-done | bytes 3670048 | tf_op jit(solution)/shard_map/all_to_all | solution.py:33
  195.4 3.0 convert_bitcast_fusion.1
  198.3 3.4 %copy.19 = f32[32,8,8,896]{3,2,0,1:T(8,128)} copy(f32[32,8,8,896]{3,2,1,0:T(8,128)S(1)} %convert_bitcast_fusion.1) | data formatting | bytes 14680064 | tf_op jit(solution)/shard_map/convert_element_type | solution.py:43
  201.8 4.5 %all-gather.9.cloned.1.call-done = bf16[1,256,28672]{2,1,0:T(8,128)(2,1)} async-done(((bf16[1,256,896]{2,1,0:T(8,128)(2,1)}), bf16[1,256,28672]{2,1,0:T(8,128)(2,1)}) %all-gather.9.cloned.1.call-update) | async-done | bytes 14680080 | tf_op jit(solution)/shard_map/all_gather | solution.py:41
  206.2 11.9 %fusion.2 = bf16[1,64,28672]{2,1,0:T(8,128)(2,1)} fusion(f32[64,28672]{1,0:T(8,128)} %bitcast.50, bf16[1,256,28672]{2,1,0:T(8,128)(2,1)} %all-gather.9.cloned.1.call-done, f32[256]{0:T(256)S(1)} %select_reduce_fusion, bf16[32,8,64]{2,1,0:T(8,128)(2,1)S(1)} %reshape.48), kind=kOutput, calls=%fused_computation.4 | convolution fusion | flops 943243264 | bytes 25723904 | tf_op jit(solution)/shard_map/dot_general | solution.py:21
  218.1 91.8 %all-gather.7.cloned.1.call-done = bf16[1,256,28672]{2,1,0:T(8,128)(2,1)} async-done(((bf16[1,256,896]{2,1,0:T(8,128)(2,1)}), bf16[1,256,28672]{2,1,0:T(8,128)(2,1)}) %all-gather.7.cloned.1.call-update) | async-done | bytes 14680080 | tf_op jit(solution)/shard_map/all_gather | solution.py:41
  309.9 0.0 copy-start
  309.9 10.2 %fusion.3 = bf16[1,64,28672]{2,1,0:T(8,128)(2,1)S(1)} fusion(f32[64,28672]{1,0:T(8,128)} %bitcast.51, bf16[1,256,28672]{2,1,0:T(8,128)(2,1)} %all-gather.7.cloned.1.call-done, f32[256]{0:T(256)S(1)} %select_reduce_fusion, bf16[32,8,64]{2,1,0:T(8,128)(2,1)S(1)} %reshape.50), kind=kOutput, calls=%fused_computation.5 | convolution fusion | flops 943243264 | bytes 25723904 | tf_op jit(solution)/shard_map/dot_general | solution.py:21
  320.2 0.0 copy-done
  320.2 3.7 %pad_maximum_fusion = bf16[2,64,28672]{2,1,0:T(8,128)(2,1)} fusion(bf16[1,64,28672]{2,1,0:T(8,128)(2,1)S(1)} %copy-done, bf16[1,64,28672]{2,1,0:T(8,128)(2,1)S(1)} %fusion.3), kind=kLoop, calls=%fused_computation.8 | loop fusion | flops 3670016 | bytes 14680064 | tf_op jit(solution)/shard_map/stack | solution.py:45
  (3 shorter events, 0.1 us)
Async XLA Ops:
  6.5 199.7 %all-gather.9.cloned.1.call-start = ((), (), s32[]{:S(2)}) async-start(), calls=%async_computation.5 | async-start | bytes 15138816 | tf_op jit(solution)/shard_map/all_gather | solution.py:41
  20.1 289.9 %all-gather.7.cloned.1.call-start = ((), (), s32[]{:S(2)}) async-start(), calls=%async_computation.4 | async-start | bytes 15138816 | tf_op jit(solution)/shard_map/all_gather | solution.py:41
  32.3 21.0 %all-to-all-start.3 = ((bf16[32,2,256]{2,1,0:T(2,128)(2,1)}), bf16[32,2,256]{2,1,0:T(2,128)(2,1)S(1)}, u32[]{:S(2)}, u32[]{:S(2)}) async-start(bf16[32,2,256]{2,1,0:T(2,128)(2,1)} %reshape.47), calls=%async_computation.3 | async-start | bytes 65536 | tf_op jit(solution)/shard_map/all_to_all | solution.py:36
  53.4 11.1 %all-to-all-start.1 = ((bf16[32,2,256]{2,1,0:T(2,128)(2,1)}), bf16[32,2,256]{2,1,0:T(2,128)(2,1)S(1)}, u32[]{:S(2)}, u32[]{:S(2)}) async-start(bf16[32,2,256]{2,1,0:T(2,128)(2,1)} %reshape.49), calls=%async_computation.1 | async-start | bytes 65536 | tf_op jit(solution)/shard_map/all_to_all | solution.py:36
  64.5 71.8 %copy-start.1 = (f32[16]{0:T(128)S(1)}, f32[16]{0:T(128)}, u32[]{:S(2)}) copy-start(f32[16]{0:T(128)} %param.7) | copy-start | bytes 196
  131.6 63.7 %all-to-all-start = ((bf16[32,64,896]{2,1,0:T(8,128)(2,1)}), bf16[32,64,896]{2,1,0:T(8,128)(2,1)}, u32[]{:S(2)}, u32[]{:S(2)}) async-start(bf16[32,64,896]{2,1,0:T(8,128)(2,1)} %bitcast.52), calls=%async_computation | async-start | bytes 7340032 | tf_op jit(solution)/shard_map/all_to_all | solution.py:33
  309.9 10.2 %copy-start = (bf16[1,64,28672]{2,1,0:T(8,128)(2,1)S(1)}, bf16[1,64,28672]{2,1,0:T(8,128)(2,1)}, u32[]{:S(2)}) copy-start(bf16[1,64,28672]{2,1,0:T(8,128)(2,1)} %fusion.2) | copy-start | bytes 11010052
Sparse Core Ops, SparseCore 0:
  20.2 185.9 all-gather.8
  207.9 101.9 all-gather.6
where the time goes:
time: 331 us
  waiting for transfers between devices  155 us (47%)
  blocking collectives  90.2 us (27%)
  starting transfers between devices  22.4 us (7%)
  matrix products  22.1 us (7%)
  local copies, waits for them, and re-layouts  17.6 us (5%)
  between operations  13.5 us (4%)
  other arithmetic  9.71 us (3%)
    all_gather x2, waiting for transfers between devices, local(): lax.all_gather(b_stacked, ('row', 'col'), axis=1, tiled=True)  96.3 us
    all_to_all x1, blocking collectives, local(): lax.all_to_all(base_tile, ('row', 'col'), split_axis=0, concat_axis=1, ti...  67.1 us
    all_to_all x1, waiting for transfers between devices, local(): lax.all_to_all(base_tile, ('row', 'col'), split_axis=0, concat_axis=1, ti...  52.2 us
    all_gather x2, blocking collectives, local(): b_stacked = lax.all_gather(up_factor_slice, 'client', axis=0, tiled=True)  23 us
    dot_general x2, matrix products, contract_ranks(): lax.dot_general(left, right, (((0,), (0,)), ((), ())), preferred_element_...  22.1 us
    all_to_all x2, starting transfers between devices, local(): lax.all_to_all(down_factor_slice, ('row', 'col'), split_axis=1, concat_ax...  17.8 us
    convert_element_type x2, local copies, waits for them, and re-layouts, local(): owned = (base_rows.astype(jnp.float32) + delta).astype(jnp.bfloat16)  6.97 us
    slice x1, local copies, waits for them, and re-layouts, local(): base_tile = frozen_up_weight[layer_index]  6.92 us
  transfers between devices with their start and end apart: 5, of which 5 were waited for; matrix products, arithmetic and copies ran while one was open for 10% of the time, Pallas kernels for 0%

commit v1 on v0

v1 whole, which is shorter than its diff:
```python
import jax
import jax.numpy as jnp
from jax import lax
from jax.experimental import pallas as pl
from jax.experimental.pallas import tpu as pltpu
from jax.sharding import PartitionSpec as P

RANK = 16
TILE_AXES = ("row", "col")
ALL_AXES = ("client", "row", "col")
RING = 4
VMEM_LIMIT = 48 * 1024 * 1024


def place_of(x, y, z, core):
    return x * 32 + ((z % 2) * 2 + core) * 8 + y * 2 + z // 2


def shift(piece, dx=0, dy=0, dz=0, dcore=0, swap_on_core_1=False):
    pairs = []
    for x in range(RING):
        for y in range(RING):
            for z in range(RING):
                for core in range(2):
                    sy, sz = (dz, dy) if swap_on_core_1 and core else (dy, dz)
                    to = place_of(
                        (x + dx) % RING, (y + sy) % RING, (z + sz) % RING, (core + dcore) % 2
                    )
                    pairs.append((place_of(x, y, z, core), to))
    return lax.ppermute(piece, ALL_AXES, pairs)


def around(piece, axis):
    return jnp.concatenate(
        [piece]
        + [shift(piece, **{axis: RING - k}, swap_on_core_1=True) for k in range(1, RING)]
    )


def gather_down(scaled_here):
    layers, ranks, rows = scaled_here.shape
    piece = scaled_here.transpose(1, 0, 2).reshape(ranks, layers * rows)
    plane = around(around(piece, "dz"), "dy")
    return plane, shift(plane, dcore=1)


def gather_up(adapter_up_stack):
    layers, ranks, cols = adapter_up_stack.shape
    piece = adapter_up_stack.transpose(1, 0, 2).reshape(ranks, layers * cols)
    after, before = shift(piece, dx=RING - 1), shift(piece, dx=1)
    half = ranks // 2
    opposite = [shift(before[:half], dx=1), shift(after[half:], dx=RING - 1)]
    return jnp.concatenate([piece, after] + opposite + [before]).reshape(32, 8, layers * cols)


def sort_kernel(b_ref, out_ref):
    row, col = lax.axis_index("row"), lax.axis_index("col")
    x, y, z, core = lax.axis_index("client"), col // 2, (col % 2) * 2 + row // 2, row % 2
    for dcore in range(2):
        holder = lax.rem(core + dcore, 2)
        for second in range(RING):
            for first in range(RING):
                dy = jnp.where(holder == 0, second, first)
                dz = jnp.where(holder == 0, first, second)
                y_from, z_from = lax.rem(y + dy, RING), lax.rem(z + dz, RING)
                group = lax.rem(z_from, 2) * 2 + holder
                block = y_from * 2 + z_from // 2
                source = lax.rem(group - x + RING, RING) * 8 + block
                slot = (dcore * RING + second) * RING + first
                out_ref[slot] = b_ref[source]


def sort_up(b_blocks):
    return pl.pallas_call(
        sort_kernel,
        out_shape=jax.ShapeDtypeStruct(b_blocks.shape, b_blocks.dtype),
        compiler_params=pltpu.CompilerParams(vmem_limit_bytes=VMEM_LIMIT),
        cost_estimate=pl.CostEstimate(flops=0, bytes_accessed=4 * b_blocks.size, transcendentals=0),
    )(b_blocks)


def merge_kernel(base_ref, a00, a01, a10, a11, b_ref, out_ref):
    cols = base_ref.shape[-1]
    for layer, (own, other) in enumerate(((a00, a01), (a10, a11))):
        left = jnp.concatenate([own[...], other[...]], axis=0)
        right = b_ref[:, layer * cols : (layer + 1) * cols]
        delta = lax.dot_general(
            left, right, (((0,), (0,)), ((), ())), preferred_element_type=jnp.float32
        )
        merged = (base_ref[layer].astype(jnp.float32) + delta).astype(jnp.bfloat16)
        out_ref[:, layer] = merged.reshape(out_ref.shape[0], *out_ref.shape[2:])


def merge(base, own, other, b_sorted, parts):
    layers, rows, cols = base.shape
    part_rows = rows // parts
    tall = 256
    steps = rows // tall
    per = tall // part_rows
    half = own.shape[0]
    a_spec = [pl.BlockSpec((half, tall), lambda i, layer=layer: (0, layer * steps + i)) for layer in range(layers)]
    return pl.pallas_call(
        merge_kernel,
        grid=(steps,),
        in_specs=[
            pl.BlockSpec((layers, tall, cols), lambda i: (0, i, 0)),
            a_spec[0],
            a_spec[0],
            a_spec[1],
            a_spec[1],
            pl.BlockSpec(b_sorted.shape, lambda i: (0, 0)),
        ],
        out_specs=pl.BlockSpec((per, layers, part_rows, cols), lambda i: (i, 0, 0, 0)),
        out_shape=jax.ShapeDtypeStruct((parts, layers, part_rows, cols), jnp.bfloat16),
        compiler_params=pltpu.CompilerParams(vmem_limit_bytes=VMEM_LIMIT),
        cost_estimate=pl.CostEstimate(
            flops=2 * layers * rows * cols * 256, bytes_accessed=4 * base.size, transcendentals=0
        ),
    )(base, own, other, own, other, b_sorted)


def settle_kernel(in_ref, out_ref):
    parts, _, _, cols = in_ref.shape
    for part in range(parts):
        out_ref[0, :, part * cols : (part + 1) * cols] = in_ref[part, 0]


def settle(received):
    parts, layers, part_rows, cols = received.shape
    tall = 16
    return pl.pallas_call(
        settle_kernel,
        grid=(layers, part_rows // tall),
        in_specs=[pl.BlockSpec((parts, 1, tall, cols), lambda l, i: (0, l, i, 0))],
        out_specs=pl.BlockSpec((1, tall, parts * cols), lambda l, i: (l, i, 0)),
        out_shape=jax.ShapeDtypeStruct((layers, part_rows, parts * cols), jnp.bfloat16),
        compiler_params=pltpu.CompilerParams(vmem_limit_bytes=VMEM_LIMIT),
        cost_estimate=pl.CostEstimate(flops=0, bytes_accessed=4 * received.size, transcendentals=0),
    )(received)


def local(frozen_up_weight, adapter_down_stack, adapter_up_stack, participant_weight):
    parts = lax.axis_size(TILE_AXES)
    ranks_here = adapter_down_stack.shape[1]
    owner = (lax.axis_index(TILE_AXES) * ranks_here) // RANK
    weight = lax.dynamic_index_in_dim(participant_weight, owner, keepdims=False)
    scaled_here = (weight * adapter_down_stack.astype(jnp.float32)).astype(jnp.bfloat16)

    own, other = gather_down(scaled_here)
    b_sorted = sort_up(gather_up(adapter_up_stack)).reshape(own.shape[0] * 2, -1)
    merged = merge(frozen_up_weight, own, other, b_sorted, parts)
    received = lax.all_to_all(merged, TILE_AXES, split_axis=0, concat_axis=0, tiled=True)
    return settle(received)


def solution(mesh):
    return jax.shard_map(
        local,
        mesh=mesh,
        in_specs=(
            P(None, "client", ("row", "col")),
            P(None, ("row", "col"), "client"),
            P(None, "client", ("row", "col")),
            P(),
        ),
        out_specs=P(None, ("client", "row", "col"), None),
        check_vma=False,
    )
```

time: 331 us -> 145 us (0.44)
  waiting for transfers between devices: 155 us -> 9.29 us
  matrix products: 22.1 us -> 0 us
  Pallas kernels: 0 us -> 18.4 us
  local copies, waits for them, and re-layouts: 17.6 us -> 2.36 us
  between operations: 13.5 us -> 0.15 us
  other arithmetic: 9.71 us -> 1.52 us
    all_gather x2 -> x0, waiting for transfers between devices: 96.3 us -> none  [local(): lax.all_gather(b_stacked, ('row', 'col'), axis=1, tiled=True)]
    all_to_all x3 -> x0, waiting for transfers between devices: 58.8 us -> none  [the longest x1 52.2 us: local(): lax.all_to_all(base_tile, ('row', 'col'), split_axis=0, concat_axis=1, ti...]
    all_to_all x1, blocking collectives: 67.1 us -> 91.1 us  [local(): lax.all_to_all(merged, TILE_AXES, split_axis=0, concat_axis=0, tiled=True)]
    all_gather x2 -> x0, blocking collectives: 23 us -> none  [local(): b_stacked = lax.all_gather(up_factor_slice, 'client', axis=0, tiled=True)]
    all_to_all x3 -> x0, starting transfers between devices: 22.4 us -> none  [the longest x2 17.8 us: local(): lax.all_to_all(down_factor_slice, ('row', 'col'), split_axis=1, concat_ax...]
    dot_general x2 -> x0, matrix products: 22.1 us -> none  [contract_ranks(): lax.dot_general(left, right, (((0,), (0,)), ((), ())), preferred_element_...]
    ppermute x0 -> x11, starting transfers between devices: none -> 19.8 us  [shift(): return lax.ppermute(piece, ALL_AXES, pairs)]
    pallas_call x0 -> x3, Pallas kernels: none -> 18.4 us  [the longest x1 9.61 us: merge(): pl.pallas_call(merge_kernel, grid=(steps,), in_specs=[pl.BlockSpec((layer...]
  transfers between devices with their start and end apart: 5 -> 11, of which waited for: 5 -> 3; matrix products, arithmetic and copies ran while one was open for 10% -> 1% of each run, Pallas kernels for 0% -> 0%
where the time goes in v1:
time: 145 us; the launch traced here: 143 us
  blocking collectives  91.1 us (63%)
  starting transfers between devices  19.8 us (14%)
  Pallas kernels  18.4 us (13%)
  waiting for transfers between devices  9.29 us (6%)
  local copies, waits for them, and re-layouts  2.36 us (2%)
  other arithmetic  1.52 us (1%)
    all_to_all x1, blocking collectives, local(): lax.all_to_all(merged, TILE_AXES, split_axis=0, concat_axis=0, tiled=True)  91.1 us
    ppermute x11, starting transfers between devices, shift(): return lax.ppermute(piece, ALL_AXES, pairs)  19.8 us
    pallas_call x1, Pallas kernels, merge(): pl.pallas_call(merge_kernel, grid=(steps,), in_specs=[pl.BlockSpec((layer...  9.61 us
    ppermute x11, waiting for transfers between devices, shift(): return lax.ppermute(piece, ALL_AXES, pairs)  9.29 us
    pallas_call x1, Pallas kernels, settle(): pl.pallas_call(settle_kernel, grid=(layers, part_rows // tall), in_specs=...  8.41 us
  transfers between devices with their start and end apart: 11, of which 3 were waited for; matrix products, arithmetic and copies ran while one was open for 1% of the time, Pallas kernels for 0%

profile of v1, /device:TPU:1, one launch (start us, length us, event | category | flops | bytes accessed | tf_op | source)
XLA Modules:
  0.0 142.7 jit_solution(12851436065703236372)
XLA Ops:
  0.0 1.2 dynamic_slice.4
  1.2 1.5 %multiply_convert_fusion = bf16[2,8,2048]{2,1,0:T(8,128)(2,1)S(1)} fusion(bf16[2,8,2048]{2,1,0:T(8,128)(2,1)} %param.5, f32[]{:T(128)} %bitcast), kind=kLoop, calls=%fused_computation.1 | loop fusion | flops 98304 | bytes 131076 | tf_op jit(solution)/shard_map/convert_element_type | solution.py:147
  2.7 2.2 %collective-permute-start.2 = (bf16[8,4096]{1,0:T(8,128)(2,1)S(1)}, bf16[8,4096]{1,0:T(8,128)(2,1)S(1)}, u32[]{:S(2)}, u32[]{:S(2)}) collective-permute-start(bf16[8,4096]{1,0:T(8,128)(2,1)S(1)} %bitcast.14), channel_id=1, source_target_pairs={{0,16},{8,10},{16,1},{24,26},{1,17},{9,11},{17,0},{25,27},{2,18},{... | collective-permute-start | bytes 196616 | tf_op jit(solution)/shard_map/ppermute | solution.py:30
  4.9 2.6 %collective-permute-start.1 = (bf16[8,4096]{1,0:T(8,128)(2,1)S(1)}, bf16[8,4096]{1,0:T(8,128)(2,1)S(1)}, u32[]{:S(2)}, u32[]{:S(2)}) collective-permute-start(bf16[8,4096]{1,0:T(8,128)(2,1)S(1)} %bitcast.15), channel_id=1, source_target_pairs={{0,1},{8,12},{16,17},{24,28},{1,0},{9,13},{17,16},{25,29},{2,3},{1... | collective-permute-start | bytes 196616 | tf_op jit(solution)/shard_map/ppermute | solution.py:30
  7.6 1.1 collective-permute-start
  8.6 1.0 copy.6
  9.6 1.3 collective-permute-start.8
  10.9 1.5 %collective-permute-start.7 = (bf16[64,1792]{1,0:T(8,128)(2,1)S(1)}, bf16[64,1792]{1,0:T(8,128)(2,1)S(1)}, u32[]{:S(2)}, u32[]{:S(2)}) collective-permute-start(bf16[64,1792]{1,0:T(8,128)(2,1)S(1)} %bitcast.12), channel_id=1, source_target_pairs={{0,96},{8,104},{16,112},{24,120},{1,97},{9,105},{17,113},{25,121},... | collective-permute-start | bytes 688136 | tf_op jit(solution)/shard_map/ppermute | solution.py:30
  12.3 0.0 collective-permute-done.2
  12.3 0.0 collective-permute-done.1
  12.4 0.0 collective-permute-done
  12.4 1.7 %collective-permute-start.5 = (bf16[32,4096]{1,0:T(8,128)(2,1)S(1)}, bf16[32,4096]{1,0:T(8,128)(2,1)S(1)}, u32[]{:S(2)}, u32[]{:S(2)}) collective-permute-start(bf16[32,4096]{1,0:T(8,128)(2,1)S(1)} %pad_maximum_fusion), channel_id=1, source_target_pairs={{0,2},{8,24},{16,18},{24,9},{1,3},{9,25},{17,19},{25,8},{2,4},{10,... | collective-permute-start | bytes 786440 | tf_op jit(solution)/shard_map/ppermute | solution.py:30
  14.1 3.3 %collective-permute-start.4 = (bf16[32,4096]{1,0:T(8,128)(2,1)S(1)}, bf16[32,4096]{1,0:T(8,128)(2,1)S(1)}, u32[]{:S(2)}, u32[]{:S(2)}) collective-permute-start(bf16[32,4096]{1,0:T(8,128)(2,1)S(1)} %pad_maximum_fusion), channel_id=1, source_target_pairs={{0,4},{8,9},{16,20},{24,25},{1,5},{9,8},{17,21},{25,24},{2,6},{10,... | collective-permute-start | bytes 786440 | tf_op jit(solution)/shard_map/ppermute | solution.py:30
  17.4 0.7 collective-permute-start.3
  18.2 5.6 %collective-permute-done.3 = bf16[32,4096]{1,0:T(8,128)(2,1)S(1)} collective-permute-done((bf16[32,4096]{1,0:T(8,128)(2,1)S(1)}, bf16[32,4096]{1,0:T(8,128)(2,1)S(1)}, u32[]{:S(2)}, u32[]{:S(2)}) %collective-permute-start.3) | collective-permute-done | bytes 262176 | tf_op jit(solution)/shard_map/ppermute | solution.py:30
  23.8 0.5 collective-permute-done.4
  24.3 0.0 collective-permute-done.5
  24.3 2.7 %collective-permute-start.6 = (bf16[128,4096]{1,0:T(8,128)(2,1)S(1)}, bf16[128,4096]{1,0:T(8,128)(2,1)S(1)}, u32[]{:S(2)}, u32[]{:S(2)}) collective-permute-start(bf16[128,4096]{1,0:T(8,128)(2,1)S(1)} %constant_dynamic-update-slice_fusion.a00.a10), channel_id=1, source_target_pairs={{0,8},{8,0},{16,24},{24,16},{1,9},{9,1},{17,25},{25,17},{2,10},{10... | collective-permute-start | bytes 3145736 | tf_op jit(solution)/shard_map/ppermute | solution.py:30
  27.0 0.0 collective-permute-done.8
  27.0 0.2 collective-permute-start.9
  27.3 0.0 collective-permute-done.7
  27.3 2.6 %collective-permute-start.10 = (bf16[32,1792]{1,0:T(8,128)(2,1)S(1)}, bf16[32,1792]{1,0:T(8,128)(2,1)S(1)}, u32[]{:S(2)}, u32[]{:S(2)}) collective-permute-start(bf16[32,1792]{1,0:T(8,128)(2,1)S(1)} %slice.9), channel_id=1, source_target_pairs={{0,96},{8,104},{16,112},{24,120},{1,97},{9,105},{17,113},{25,121},... | collective-permute-start | bytes 344072 | tf_op jit(solution)/shard_map/ppermute | solution.py:30
  29.9 3.2 %collective-permute-done.9 = bf16[32,1792]{1,0:T(8,128)(2,1)S(1)} collective-permute-done((bf16[32,1792]{1,0:T(8,128)(2,1)S(1)}, bf16[32,1792]{1,0:T(8,128)(2,1)S(1)}, u32[]{:S(2)}, u32[]{:S(2)}) %collective-permute-start.9) | collective-permute-done | bytes 114720 | tf_op jit(solution)/shard_map/ppermute | solution.py:30
  33.1 0.0 collective-permute-done.10
  33.1 0.4 shard_map.46
  33.6 0.0 collective-permute-done.6.a01.a11
  33.6 9.6 %shard_map.47 = bf16[32,2,64,896]{3,2,1,0:T(8,128)(2,1)} custom-call(bf16[2,2048,896]{2,1,0:T(8,128)(2,1)} %base_ref.1, bf16[128,4096]{1,0:T(8,128)(2,1)S(1)} %constant_dynamic-update-slice_fusion.a00.a10, bf16[128,4096]{1,0:T(8,128)(2,1)S(1)} %collective-permute-done.6.a01.a11, bf16[128,4096]{1,0:T(8,128)(2,1)S(1)} %constant_dynamic-update-slice_fusion.a00.a10, ...), custom_call_target="tpu_custom_call" | custom-call | flops 1879048192 | bytes 14680064 | tf_op jit(solution)/shard_map/pallas_call | solution.py:102
  43.2 91.1 %all_to_all.5.in_ref = bf16[32,2,64,896]{3,2,1,0:T(8,128)(2,1)} all-to-all(bf16[32,2,64,896]{3,2,1,0:T(8,128)(2,1)} %shard_map.47), channel_id=1, replica_groups=mesh['client'=4,'row'=4,'col'=8] {'row','col'}, dimensions={0} | all-to-all | bytes 14680064 | tf_op jit(solution)/shard_map/all_to_all | solution.py:152
  134.3 8.4 %shard_map.48 = bf16[2,64,28672]{2,1,0:T(8,128)(2,1)} custom-call(bf16[32,2,64,896]{3,2,1,0:T(8,128)(2,1)} %all_to_all.5.in_ref), custom_call_target="tpu_custom_call" | custom-call | bytes 14680064 | tf_op jit(solution)/shard_map/pallas_call | solution.py:131
  (15 shorter events, 0.2 us)
Async XLA Ops:
  2.7 9.6 %collective-permute-start.2 = (bf16[8,4096]{1,0:T(8,128)(2,1)S(1)}, bf16[8,4096]{1,0:T(8,128)(2,1)S(1)}, u32[]{:S(2)}, u32[]{:S(2)}) collective-permute-start(bf16[8,4096]{1,0:T(8,128)(2,1)S(1)} %bitcast.14), channel_id=1, source_target_pairs={{0,16},{8,10},{16,1},{24,26},{1,17},{9,11},{17,0},{25,27},{2,18},{... | collective-permute-start | bytes 196616 | tf_op jit(solution)/shard_map/ppermute | solution.py:30
  4.9 7.4 %collective-permute-start.1 = (bf16[8,4096]{1,0:T(8,128)(2,1)S(1)}, bf16[8,4096]{1,0:T(8,128)(2,1)S(1)}, u32[]{:S(2)}, u32[]{:S(2)}) collective-permute-start(bf16[8,4096]{1,0:T(8,128)(2,1)S(1)} %bitcast.15), channel_id=1, source_target_pairs={{0,1},{8,12},{16,17},{24,28},{1,0},{9,13},{17,16},{25,29},{2,3},{1... | collective-permute-start | bytes 196616 | tf_op jit(solution)/shard_map/ppermute | solution.py:30
  7.6 4.8 %collective-permute-start = (bf16[8,4096]{1,0:T(8,128)(2,1)S(1)}, bf16[8,4096]{1,0:T(8,128)(2,1)S(1)}, u32[]{:S(2)}, u32[]{:S(2)}) collective-permute-start(bf16[8,4096]{1,0:T(8,128)(2,1)S(1)} %bitcast.16), channel_id=1, source_target_pairs={{0,17},{8,14},{16,0},{24,30},{1,16},{9,15},{17,1},{25,31},{2,19},{... | collective-permute-start | bytes 196616 | tf_op jit(solution)/shard_map/ppermute | solution.py:30
  9.6 17.4 %collective-permute-start.8 = (bf16[64,1792]{1,0:T(8,128)(2,1)S(1)}, bf16[64,1792]{1,0:T(8,128)(2,1)S(1)}, u32[]{:S(2)}, u32[]{:S(2)}) collective-permute-start(bf16[64,1792]{1,0:T(8,128)(2,1)S(1)} %bitcast.11), channel_id=1, source_target_pairs={{0,32},{8,40},{16,48},{24,56},{1,33},{9,41},{17,49},{25,57},{2,34}... | collective-permute-start | bytes 688136 | tf_op jit(solution)/shard_map/ppermute | solution.py:30
  10.9 16.4 %collective-permute-start.7 = (bf16[64,1792]{1,0:T(8,128)(2,1)S(1)}, bf16[64,1792]{1,0:T(8,128)(2,1)S(1)}, u32[]{:S(2)}, u32[]{:S(2)}) collective-permute-start(bf16[64,1792]{1,0:T(8,128)(2,1)S(1)} %bitcast.12), channel_id=1, source_target_pairs={{0,96},{8,104},{16,112},{24,120},{1,97},{9,105},{17,113},{25,121},... | collective-permute-start | bytes 688136 | tf_op jit(solution)/shard_map/ppermute | solution.py:30
  12.4 11.9 %collective-permute-start.5 = (bf16[32,4096]{1,0:T(8,128)(2,1)S(1)}, bf16[32,4096]{1,0:T(8,128)(2,1)S(1)}, u32[]{:S(2)}, u32[]{:S(2)}) collective-permute-start(bf16[32,4096]{1,0:T(8,128)(2,1)S(1)} %pad_maximum_fusion), channel_id=1, source_target_pairs={{0,2},{8,24},{16,18},{24,9},{1,3},{9,25},{17,19},{25,8},{2,4},{10,... | collective-permute-start | bytes 786440 | tf_op jit(solution)/shard_map/ppermute | solution.py:30
  14.1 10.2 %collective-permute-start.4 = (bf16[32,4096]{1,0:T(8,128)(2,1)S(1)}, bf16[32,4096]{1,0:T(8,128)(2,1)S(1)}, u32[]{:S(2)}, u32[]{:S(2)}) collective-permute-start(bf16[32,4096]{1,0:T(8,128)(2,1)S(1)} %pad_maximum_fusion), channel_id=1, source_target_pairs={{0,4},{8,9},{16,20},{24,25},{1,5},{9,8},{17,21},{25,24},{2,6},{10,... | collective-permute-start | bytes 786440 | tf_op jit(solution)/shard_map/ppermute | solution.py:30
  17.4 6.3 %collective-permute-start.3 = (bf16[32,4096]{1,0:T(8,128)(2,1)S(1)}, bf16[32,4096]{1,0:T(8,128)(2,1)S(1)}, u32[]{:S(2)}, u32[]{:S(2)}) collective-permute-start(bf16[32,4096]{1,0:T(8,128)(2,1)S(1)} %pad_maximum_fusion), channel_id=1, source_target_pairs={{0,6},{8,25},{16,22},{24,8},{1,7},{9,24},{17,23},{25,9},{2,0},{10,... | collective-permute-start | bytes 786440 | tf_op jit(solution)/shard_map/ppermute | solution.py:30
  24.3 9.2 %collective-permute-start.6 = (bf16[128,4096]{1,0:T(8,128)(2,1)S(1)}, bf16[128,4096]{1,0:T(8,128)(2,1)S(1)}, u32[]{:S(2)}, u32[]{:S(2)}) collective-permute-start(bf16[128,4096]{1,0:T(8,128)(2,1)S(1)} %constant_dynamic-update-slice_fusion.a00.a10), channel_id=1, source_target_pairs={{0,8},{8,0},{16,24},{24,16},{1,9},{9,1},{17,25},{25,17},{2,10},{10... | collective-permute-start | bytes 3145736 | tf_op jit(solution)/shard_map/ppermute | solution.py:30
  27.0 6.0 %collective-permute-start.9 = (bf16[32,1792]{1,0:T(8,128)(2,1)S(1)}, bf16[32,1792]{1,0:T(8,128)(2,1)S(1)}, u32[]{:S(2)}, u32[]{:S(2)}) collective-permute-start(bf16[32,1792]{1,0:T(8,128)(2,1)S(1)} %slice.8), channel_id=1, source_target_pairs={{0,32},{8,40},{16,48},{24,56},{1,33},{9,41},{17,49},{25,57},{2,34}... | collective-permute-start | bytes 344072 | tf_op jit(solution)/shard_map/ppermute | solution.py:30
  27.3 5.8 %collective-permute-start.10 = (bf16[32,1792]{1,0:T(8,128)(2,1)S(1)}, bf16[32,1792]{1,0:T(8,128)(2,1)S(1)}, u32[]{:S(2)}, u32[]{:S(2)}) collective-permute-start(bf16[32,1792]{1,0:T(8,128)(2,1)S(1)} %slice.9), channel_id=1, source_target_pairs={{0,96},{8,104},{16,112},{24,120},{1,97},{9,105},{17,113},{25,121},... | collective-permute-start | bytes 344072 | tf_op jit(solution)/shard_map/ppermute | solution.py:30

commit v2 on v1

v2 whole, which is shorter than its diff:
```python
import jax
import jax.numpy as jnp
from jax import lax
from jax.experimental import pallas as pl
from jax.experimental.pallas import tpu as pltpu
from jax.sharding import PartitionSpec as P

RANK = 16
TILE_AXES = ("row", "col")
ALL_AXES = ("client", "row", "col")
RING = 4
BLOCKS = 32
VMEM_LIMIT = 16 * 1024 * 1024


def place_of(x, y, z, core):
    return x * 32 + ((z % 2) * 2 + core) * 8 + y * 2 + z // 2


def spot_of(y, z, core):
    return (y % 2) * 16 + (y // 2) * 8 + (z // 2) * 4 + (z % 2) * 2 + core


def exchange(pieces):
    group = [0] * BLOCKS
    for y in range(RING):
        for z in range(RING):
            for core in range(2):
                group[spot_of(y, z, core)] = place_of(0, y, z, core)
    return lax.all_to_all(
        pieces, TILE_AXES, split_axis=0, concat_axis=0, axis_index_groups=[group], tiled=True
    )


def shift(piece, dx=0, dy=0, dz=0, dcore=0, swap_on_core_1=False):
    pairs = []
    for x in range(RING):
        for y in range(RING):
            for z in range(RING):
                for core in range(2):
                    sy, sz = (dz, dy) if swap_on_core_1 and core else (dy, dz)
                    to = place_of(
                        (x + dx) % RING, (y + sy) % RING, (z + sz) % RING, (core + dcore) % 2
                    )
                    pairs.append((place_of(x, y, z, core), to))
    return lax.ppermute(piece, ALL_AXES, pairs)


def around(piece, axis):
    return [piece] + [
        shift(piece, **{axis: RING - k}, swap_on_core_1=True) for k in range(1, RING)
    ]


def gather(base, adapter_down_stack, adapter_up_stack):
    layers, ranks, cols = adapter_up_stack.shape
    up = adapter_up_stack.reshape(1, layers, ranks // 8, 8, cols)
    near_up = jnp.concatenate([shift(up, dx=RING - 1), shift(up, dx=1)])
    touched = touch(base)
    mine, *others = around(adapter_down_stack[None], "dz")
    near_up, *others = gate([near_up] + others, [touched])
    ring = jnp.concatenate([mine] + others)
    own = around(ring, "dy")
    far_up = shift(up, dx=2)
    other = [shift(piece, dcore=1) for piece in own]
    b_groups = jnp.concatenate([up, near_up, far_up])
    return own + other, b_groups


def touch_kernel(base_ref, out_ref):
    out_ref[...] = jnp.zeros(out_ref.shape, out_ref.dtype)


def touch(base):
    vmem = pl.BlockSpec(memory_space=pltpu.VMEM)
    return pl.pallas_call(
        touch_kernel,
        in_specs=[vmem],
        out_specs=vmem,
        out_shape=jax.ShapeDtypeStruct((8, 128), jnp.float32),
        compiler_params=pltpu.CompilerParams(vmem_limit_bytes=VMEM_LIMIT),
        cost_estimate=pl.CostEstimate(flops=0, bytes_accessed=4 * base.size, transcendentals=0),
    )(base)


def gate(values, after):
    anywhere = pl.BlockSpec(memory_space=pl.ANY)
    specs = [anywhere] * len(values)
    return pl.pallas_call(
        lambda *refs: None,
        in_specs=specs + [anywhere] * len(after),
        out_specs=specs,
        out_shape=[jax.ShapeDtypeStruct(v.shape, v.dtype) for v in values],
        input_output_aliases={i: i for i in range(len(values))},
        compiler_params=pltpu.CompilerParams(vmem_limit_bytes=VMEM_LIMIT),
        cost_estimate=pl.CostEstimate(flops=0, bytes_accessed=0, transcendentals=0),
    )(*values, *after)


def sort_kernel(weight_ref, b_ref, out_ref, scale_ref):
    row, col = lax.axis_index("row"), lax.axis_index("col")
    x, y, z, core = lax.axis_index("client"), col // 2, (col % 2) * 2 + row // 2, row % 2
    for dcore in range(2):
        holder = lax.rem(core + dcore, 2)
        for second in range(RING):
            for first in range(RING):
                dy = jnp.where(holder == 0, second, first)
                dz = jnp.where(holder == 0, first, second)
                y_from, z_from = lax.rem(y + dy, RING), lax.rem(z + dz, RING)
                group = lax.rem(z_from, 2) * 2 + holder
                block = y_from * 2 + z_from // 2
                slot = (dcore * RING + second) * RING + first
                ahead = lax.rem(group - x + RING, RING)
                out_ref[:, slot] = b_ref[jnp.where(ahead < 2, ahead, 5 - ahead), :, block]
                scale_ref[slot] = jnp.full(
                    scale_ref.shape[1:], weight_ref[group * 4 + block // 2], jnp.float32
                )


def sort_up(participant_weight, b_groups):
    _, layers, _, _, cols = b_groups.shape
    vmem = pl.BlockSpec(memory_space=pltpu.VMEM)
    return pl.pallas_call(
        sort_kernel,
        in_specs=[pl.BlockSpec(memory_space=pltpu.SMEM), vmem],
        out_specs=[vmem, vmem],
        out_shape=[
            jax.ShapeDtypeStruct((layers, BLOCKS, 8, cols), b_groups.dtype),
            jax.ShapeDtypeStruct((BLOCKS, 8, 128), jnp.float32),
        ],
        compiler_params=pltpu.CompilerParams(vmem_limit_bytes=VMEM_LIMIT),
        cost_estimate=pl.CostEstimate(flops=0, bytes_accessed=4 * b_groups.size, transcendentals=0),
    )(participant_weight, b_groups)


def merge_kernel(base_ref, *refs):
    a_refs, (b_ref, scale_ref, out_ref) = refs[:-3], refs[-3:]
    layers, rows, cols = base_ref.shape
    part_rows = out_ref.shape[2]
    tall = 256
    per = tall // part_rows
    ranks = BLOCKS * 8
    scale = scale_ref[...].reshape(ranks, 128)
    scale = jnp.concatenate([scale] * (tall // 128), axis=1)
    for layer in range(layers):
        right = b_ref[layer].reshape(ranks, cols)

        @pl.loop(0, rows // tall, unroll=4)
        def _(i):
            span = pl.ds(pl.multiple_of(i * tall, tall), tall)
            left = jnp.concatenate(
                [ref[:, layer, :, span].reshape(-1, tall) for ref in a_refs]
            )
            left = (scale * left.astype(jnp.float32)).astype(jnp.bfloat16)
            delta = lax.dot_general(
                left, right, (((0,), (0,)), ((), ())), preferred_element_type=jnp.float32
            )
            merged = (base_ref[layer, span].astype(jnp.float32) + delta).astype(jnp.bfloat16)
            for part in range(per):
                place = i * per + part
                row, col = place // 8, lax.rem(place, 8)
                spot = spot_of(col // 2, lax.rem(col, 2) * 2 + row // 2, lax.rem(row, 2))
                out_ref[spot, layer] = merged[part * part_rows : (part + 1) * part_rows]


def merge(base, a_pieces, b_sorted, scale, parts):
    layers, rows, cols = base.shape
    vmem = pl.BlockSpec(memory_space=pltpu.VMEM)
    return pl.pallas_call(
        merge_kernel,
        in_specs=[vmem] * (len(a_pieces) + 3),
        out_specs=vmem,
        out_shape=jax.ShapeDtypeStruct((parts, layers, rows // parts, cols), jnp.bfloat16),
        compiler_params=pltpu.CompilerParams(vmem_limit_bytes=VMEM_LIMIT),
        cost_estimate=pl.CostEstimate(
            flops=2 * layers * rows * cols * 256, bytes_accessed=4 * base.size, transcendentals=0
        ),
    )(base, *a_pieces, b_sorted, scale)


def settle_kernel(in_ref, out_ref, sems):
    parts, layers, _, cols = in_ref.shape
    copies = [
        pltpu.make_async_copy(
            in_ref.at[spot_of(y, z, core), layer],
            out_ref.at[layer, :, pl.ds(place_of(0, y, z, core) * cols, cols)],
            sems.at[spot_of(y, z, core), layer],
        )
        for y in range(RING)
        for z in range(RING)
        for core in range(2)
        for layer in range(layers)
    ]
    for copy in copies:
        copy.start()
    for copy in copies:
        copy.wait()


def settle(received):
    parts, layers, part_rows, cols = received.shape
    return pl.pallas_call(
        settle_kernel,
        in_specs=[pl.BlockSpec(memory_space=pltpu.VMEM)],
        out_specs=pl.BlockSpec(memory_space=pl.ANY),
        out_shape=jax.ShapeDtypeStruct((layers, part_rows, parts * cols), jnp.bfloat16),
        scratch_shapes=[pltpu.SemaphoreType.DMA((parts, layers))],
        compiler_params=pltpu.CompilerParams(vmem_limit_bytes=VMEM_LIMIT),
        cost_estimate=pl.CostEstimate(flops=0, bytes_accessed=4 * received.size, transcendentals=0),
    )(received)


def local(frozen_up_weight, adapter_down_stack, adapter_up_stack, participant_weight):
    parts = lax.axis_size(TILE_AXES)
    a_pieces, b_groups = gather(frozen_up_weight, adapter_down_stack, adapter_up_stack)
    b_sorted, scale = sort_up(participant_weight, b_groups)
    merged = merge(frozen_up_weight, a_pieces, b_sorted, scale, parts)
    return settle(exchange(merged))


def solution(mesh):
    return jax.shard_map(
        local,
        mesh=mesh,
        in_specs=(
            P(None, "client", ("row", "col")),
            P(None, ("row", "col"), "client"),
            P(None, "client", ("row", "col")),
            P(),
        ),
        out_specs=P(None, ("client", "row", "col"), None),
        check_vma=False,
    )
```

time: 145 us -> 125 us (0.86); the launches traced: 143 us -> 125 us
  Pallas kernels: 18.4 us -> 8 us
  waiting for transfers between devices: 9.29 us -> 1.63 us
  starting transfers between devices: 19.8 us -> 21.6 us
    pallas_call x3 -> x5, Pallas kernels: 18.4 us -> 8 us  [the longest x1 3.49 us: settle(): pl.pallas_call(settle_kernel, in_specs=[pl.BlockSpec(memory_space=pltpu.V...]
    ppermute x11 -> x13, waiting for transfers between devices: 9.29 us -> 1.63 us  [shift(): return lax.ppermute(piece, ALL_AXES, pairs)]
    unnamed x10, local copies, waits for them, and re-layouts: 0.11 us -> 3.8 us
    ppermute x11 -> x13, starting transfers between devices: 19.8 us -> 21.6 us  [shift(): return lax.ppermute(piece, ALL_AXES, pairs)]
    convert_element_type x1 -> x0, other arithmetic: 1.5 us -> none  [local(): (weight * adapter_down_stack.astype(jnp.float32)).astype(jnp.bfloat16)]
  transfers between devices with their start and end apart: 11 -> 13, of which waited for: 3 -> 2; matrix products, arithmetic and copies ran while one was open for 1% -> 0% of each run, Pallas kernels for 0% -> 1%
where the time goes in v2:
time: 125 us
  blocking collectives  90 us (72%)
  starting transfers between devices  21.6 us (17%)
  Pallas kernels  8 us (6%)
  local copies, waits for them, and re-layouts  3.8 us (3%)
  waiting for transfers between devices  1.63 us (1%)
    all_to_all x1, blocking collectives, exchange(): lax.all_to_all(pieces, TILE_AXES, split_axis=0, concat_axis=0, axis_index...  90 us
    ppermute x13, starting transfers between devices, shift(): return lax.ppermute(piece, ALL_AXES, pairs)  21.6 us
    unnamed x10, local copies, waits for them, and re-layouts  3.8 us
    pallas_call x1, Pallas kernels, settle(): pl.pallas_call(settle_kernel, in_specs=[pl.BlockSpec(memory_space=pltpu.V...  3.49 us
    pallas_call x1, Pallas kernels, merge(): pl.pallas_call(merge_kernel, in_specs=[vmem] * (len(a_pieces) + 3), out_s...  3.37 us
  transfers between devices with their start and end apart: 13, of which 2 were waited for; matrix products, arithmetic and copies ran while one was open for 0% of the time, Pallas kernels for 1%

profile of v2, /device:TPU:1, one launch (start us, length us, event | category | flops | bytes accessed | tf_op | source)
XLA Modules:
  0.0 125.3 jit_solution(8107160511807991397)
XLA Ops:
  0.0 0.0 copy-start.2
  0.0 2.0 %collective-permute-start.1 = (bf16[1,2,8,8,896]{4,3,2,1,0:T(8,128)(2,1)}, bf16[1,2,8,8,896]{4,3,2,1,0:T(8,128)(2,1)S(1)}, u32[]{:S(2)}, u32[]{:S(2)}) collective-permute-start(bf16[1,2,8,8,896]{4,3,2,1,0:T(8,128)(2,1)} %bitcast.2), channel_id=1, source_target_pairs={{0,32},{8,40},{16,48},{24,56},{1,33},{9,41},{17,49},{25,57},{2,34}... | collective-permute-start | bytes 688136 | tf_op jit(solution)/shard_map/ppermute | solution.py:46
  2.0 1.3 %collective-permute-start = (bf16[1,2,8,8,896]{4,3,2,1,0:T(8,128)(2,1)}, bf16[1,2,8,8,896]{4,3,2,1,0:T(8,128)(2,1)S(1)}, u32[]{:S(2)}, u32[]{:S(2)}) collective-permute-start(bf16[1,2,8,8,896]{4,3,2,1,0:T(8,128)(2,1)} %bitcast.3), channel_id=1, source_target_pairs={{0,96},{8,104},{16,112},{24,120},{1,97},{9,105},{17,113},{25,121},... | collective-permute-start | bytes 688136 | tf_op jit(solution)/shard_map/ppermute | solution.py:46
  3.4 1.4 %collective-permute-start.4 = (bf16[1,2,8,2048]{3,2,1,0:T(8,128)(2,1)}, bf16[1,2,8,2048]{3,2,1,0:T(8,128)(2,1)S(1)}, u32[]{:S(2)}, u32[]{:S(2)}) collective-permute-start(bf16[1,2,8,2048]{3,2,1,0:T(8,128)(2,1)} %bitcast.6), channel_id=1, source_target_pairs={{0,16},{8,10},{16,1},{24,26},{1,17},{9,11},{17,0},{25,27},{2,18},{... | collective-permute-start | bytes 196616 | tf_op jit(solution)/shard_map/ppermute | solution.py:46
  4.8 2.6 %collective-permute-start.3 = (bf16[1,2,8,2048]{3,2,1,0:T(8,128)(2,1)}, bf16[1,2,8,2048]{3,2,1,0:T(8,128)(2,1)S(1)}, u32[]{:S(2)}, u32[]{:S(2)}) collective-permute-start(bf16[1,2,8,2048]{3,2,1,0:T(8,128)(2,1)} %bitcast.7), channel_id=1, source_target_pairs={{0,1},{8,12},{16,17},{24,28},{1,0},{9,13},{17,16},{25,29},{2,3},{1... | collective-permute-start | bytes 196616 | tf_op jit(solution)/shard_map/ppermute | solution.py:46
  7.4 1.1 collective-permute-start.2
  8.5 0.0 copy-start
  8.5 3.1 %copy-done = bf16[2,2048,896]{2,1,0:T(8,128)(2,1)S(1)} copy-done((bf16[2,2048,896]{2,1,0:T(8,128)(2,1)S(1)}, bf16[2,2048,896]{2,1,0:T(8,128)(2,1)}, u32[]{:S(2)}) %copy-start) | copy-done | bytes 7340056
  11.6 0.0 copy-start.4
  11.6 0.0 copy-start.3
  11.6 0.0 copy-start.1
  11.6 0.0 collective-permute-done.1
  11.6 0.0 collective-permute-done
  11.6 0.1 pad_maximum_fusion.1.refs_0_
  11.7 0.0 collective-permute-done.4.refs_3_
  11.7 0.0 collective-permute-done.3.refs_2_
  11.7 0.0 collective-permute-done.2.refs_1_
  11.7 0.7 copy-done.4
  12.5 1.7 %collective-permute-start.7 = (bf16[4,2,8,2048]{3,2,1,0:T(8,128)(2,1)S(1)}, bf16[4,2,8,2048]{3,2,1,0:T(8,128)(2,1)S(1)}, u32[]{:S(2)}, u32[]{:S(2)}) collective-permute-start(bf16[4,2,8,2048]{3,2,1,0:T(8,128)(2,1)S(1)} %pad_maximum_fusion.2.refs_0_), channel_id=1, source_target_pairs={{0,2},{8,24},{16,18},{24,9},{1,3},{9,25},{17,19},{25,8},{2,4},{10,... | collective-permute-start | bytes 786440 | tf_op jit(solution)/shard_map/ppermute | solution.py:46
  14.2 3.3 %collective-permute-start.6 = (bf16[4,2,8,2048]{3,2,1,0:T(8,128)(2,1)S(1)}, bf16[4,2,8,2048]{3,2,1,0:T(8,128)(2,1)S(1)}, u32[]{:S(2)}, u32[]{:S(2)}) collective-permute-start(bf16[4,2,8,2048]{3,2,1,0:T(8,128)(2,1)S(1)} %pad_maximum_fusion.2.refs_0_), channel_id=1, source_target_pairs={{0,4},{8,9},{16,20},{24,25},{1,5},{9,8},{17,21},{25,24},{2,6},{10,... | collective-permute-start | bytes 786440 | tf_op jit(solution)/shard_map/ppermute | solution.py:46
  17.5 0.7 collective-permute-start.5
  18.2 0.0 copy-done.3
  18.2 1.5 %collective-permute-start.12 = (bf16[1,2,8,8,896]{4,3,2,1,0:T(8,128)(2,1)S(1)}, bf16[1,2,8,8,896]{4,3,2,1,0:T(8,128)(2,1)S(1)}, u32[]{:S(2)}, u32[]{:S(2)}) collective-permute-start(bf16[1,2,8,8,896]{4,3,2,1,0:T(8,128)(2,1)S(1)} %bitcast.4), channel_id=1, source_target_pairs={{0,64},{8,72},{16,80},{24,88},{1,65},{9,73},{17,81},{25,89},{2,66}... | collective-permute-start | bytes 688136 | tf_op jit(solution)/shard_map/ppermute | solution.py:46
  19.7 3.2 %collective-permute-start.8 = (bf16[4,2,8,2048]{3,2,1,0:T(8,128)(2,1)S(1)}, bf16[4,2,8,2048]{3,2,1,0:T(8,128)(2,1)S(1)}, u32[]{:S(2)}, u32[]{:S(2)}) collective-permute-start(bf16[4,2,8,2048]{3,2,1,0:T(8,128)(2,1)S(1)} %pad_maximum_fusion.2.refs_0_), channel_id=1, source_target_pairs={{0,8},{8,0},{16,24},{24,16},{1,9},{9,1},{17,25},{25,17},{2,10},{10... | collective-permute-start | bytes 786440 | tf_op jit(solution)/shard_map/ppermute | solution.py:46
  22.9 0.0 collective-permute-done.7.refs_3_
  22.9 0.0 collective-permute-start.11
  22.9 1.4 %collective-permute-done.6.refs_2_ = bf16[4,2,8,2048]{3,2,1,0:T(8,128)(2,1)S(1)} collective-permute-done((bf16[4,2,8,2048]{3,2,1,0:T(8,128)(2,1)S(1)}, bf16[4,2,8,2048]{3,2,1,0:T(8,128)(2,1)S(1)}, u32[]{:S(2)}, u32[]{:S(2)}) %collective-permute-start.6) | collective-permute-done | bytes 262176 | tf_op jit(solution)/shard_map/ppermute | solution.py:46
  24.3 2.6 %collective-permute-start.10 = (bf16[4,2,8,2048]{3,2,1,0:T(8,128)(2,1)S(1)}, bf16[4,2,8,2048]{3,2,1,0:T(8,128)(2,1)S(1)}, u32[]{:S(2)}, u32[]{:S(2)}) collective-permute-start(bf16[4,2,8,2048]{3,2,1,0:T(8,128)(2,1)S(1)} %collective-permute-done.6.refs_2_), channel_id=1, source_target_pairs={{0,8},{8,0},{16,24},{24,16},{1,9},{9,1},{17,25},{25,17},{2,10},{10... | collective-permute-start | bytes 786440 | tf_op jit(solution)/shard_map/ppermute | solution.py:46
  26.9 0.0 collective-permute-done.5.refs_1_
  26.9 0.0 collective-permute-start.9
  26.9 0.0 collective-permute-done.12
  26.9 0.1 pad_maximum_fusion.b_ref
  27.1 0.0 copy-done.2
  27.1 1.1 shard_map.48
  28.2 0.0 collective-permute-done.8.refs_4_
  28.2 0.0 collective-permute-done.11.refs_7_
  28.2 0.0 collective-permute-done.10.refs_6_
  28.2 0.2 collective-permute-done.9.refs_5_
  28.5 0.0 copy-done.1
  28.5 3.4 %shard_map.49 = bf16[32,2,64,896]{3,2,1,0:T(8,128)(2,1)S(1)} custom-call(bf16[2,2048,896]{2,1,0:T(8,128)(2,1)S(1)} %copy-done.1, bf16[4,2,8,2048]{3,2,1,0:T(8,128)(2,1)S(1)} %pad_maximum_fusion.2.refs_0_, bf16[4,2,8,2048]{3,2,1,0:T(8,128)(2,1)S(1)} %collective-permute-done.5.refs_1_, bf16[4,2,8,2048]{3,2,1,0:T(8,128)(2,1)S(1)} %collective-permute-done.6.refs_2_, ...), custom_call_target="tpu_custom_call" | custom-call | flops 1879048192 | bytes 14680064 | tf_op jit(solution)/shard_map/pallas_call | solution.py:169
  31.8 90.0 %all_to_all.5.in_ref = bf16[32,2,64,896]{3,2,1,0:T(8,128)(2,1)S(1)} all-to-all(bf16[32,2,64,896]{3,2,1,0:T(8,128)(2,1)S(1)} %shard_map.49), channel_id=1, replica_groups={{0,8,16,24,1,9,17,25,4,12,20,28,5,13,21,29,2,10,18,26,3,11,19,27,6,14,2..., dimensions={0} | all-to-all | bytes 14680064 | tf_op jit(solution)/shard_map/all_to_all | solution.py:30
  121.8 3.5 %shard_map.50 = bf16[2,64,28672]{2,1,0:T(8,128)(2,1)} custom-call(bf16[32,2,64,896]{3,2,1,0:T(8,128)(2,1)S(1)} %all_to_all.5.in_ref), custom_call_target="tpu_custom_call" | custom-call | bytes 14680064 | tf_op jit(solution)/shard_map/pallas_call | solution.py:202
  (3 shorter events, 0.0 us)
Async XLA Ops:
  0.0 27.1 %copy-start.2 = (f32[16]{0:T(128)S(1)}, f32[16]{0:T(128)}, u32[]{:S(2)}) copy-start(f32[16]{0:T(128)} %weight_ref.1) | copy-start | bytes 196
  0.0 11.6 %collective-permute-start.1 = (bf16[1,2,8,8,896]{4,3,2,1,0:T(8,128)(2,1)}, bf16[1,2,8,8,896]{4,3,2,1,0:T(8,128)(2,1)S(1)}, u32[]{:S(2)}, u32[]{:S(2)}) collective-permute-start(bf16[1,2,8,8,896]{4,3,2,1,0:T(8,128)(2,1)} %bitcast.2), channel_id=1, source_target_pairs={{0,32},{8,40},{16,48},{24,56},{1,33},{9,41},{17,49},{25,57},{2,34}... | collective-permute-start | bytes 688136 | tf_op jit(solution)/shard_map/ppermute | solution.py:46
  2.0 9.6 %collective-permute-start = (bf16[1,2,8,8,896]{4,3,2,1,0:T(8,128)(2,1)}, bf16[1,2,8,8,896]{4,3,2,1,0:T(8,128)(2,1)S(1)}, u32[]{:S(2)}, u32[]{:S(2)}) collective-permute-start(bf16[1,2,8,8,896]{4,3,2,1,0:T(8,128)(2,1)} %bitcast.3), channel_id=1, source_target_pairs={{0,96},{8,104},{16,112},{24,120},{1,97},{9,105},{17,113},{25,121},... | collective-permute-start | bytes 688136 | tf_op jit(solution)/shard_map/ppermute | solution.py:46
  3.4 8.3 %collective-permute-start.4 = (bf16[1,2,8,2048]{3,2,1,0:T(8,128)(2,1)}, bf16[1,2,8,2048]{3,2,1,0:T(8,128)(2,1)S(1)}, u32[]{:S(2)}, u32[]{:S(2)}) collective-permute-start(bf16[1,2,8,2048]{3,2,1,0:T(8,128)(2,1)} %bitcast.6), channel_id=1, source_target_pairs={{0,16},{8,10},{16,1},{24,26},{1,17},{9,11},{17,0},{25,27},{2,18},{... | collective-permute-start | bytes 196616 | tf_op jit(solution)/shard_map/ppermute | solution.py:46
  4.8 6.9 %collective-permute-start.3 = (bf16[1,2,8,2048]{3,2,1,0:T(8,128)(2,1)}, bf16[1,2,8,2048]{3,2,1,0:T(8,128)(2,1)S(1)}, u32[]{:S(2)}, u32[]{:S(2)}) collective-permute-start(bf16[1,2,8,2048]{3,2,1,0:T(8,128)(2,1)} %bitcast.7), channel_id=1, source_target_pairs={{0,1},{8,12},{16,17},{24,28},{1,0},{9,13},{17,16},{25,29},{2,3},{1... | collective-permute-start | bytes 196616 | tf_op jit(solution)/shard_map/ppermute | solution.py:46
  7.4 4.3 %collective-permute-start.2 = (bf16[1,2,8,2048]{3,2,1,0:T(8,128)(2,1)}, bf16[1,2,8,2048]{3,2,1,0:T(8,128)(2,1)S(1)}, u32[]{:S(2)}, u32[]{:S(2)}) collective-permute-start(bf16[1,2,8,2048]{3,2,1,0:T(8,128)(2,1)} %bitcast.8), channel_id=1, source_target_pairs={{0,17},{8,14},{16,0},{24,30},{1,16},{9,15},{17,1},{25,31},{2,19},{... | collective-permute-start | bytes 196616 | tf_op jit(solution)/shard_map/ppermute | solution.py:46
  8.5 3.1 %copy-start = (bf16[2,2048,896]{2,1,0:T(8,128)(2,1)S(1)}, bf16[2,2048,896]{2,1,0:T(8,128)(2,1)}, u32[]{:S(2)}) copy-start(bf16[2,2048,896]{2,1,0:T(8,128)(2,1)} %base_ref.3) | copy-start | bytes 22020100
  11.6 0.8 copy-start.4
  11.6 6.6 %copy-start.3 = (bf16[2,64,896]{2,1,0:T(8,128)(2,1)S(1)}, bf16[2,64,896]{2,1,0:T(8,128)(2,1)}, u32[]{:S(2)}) copy-start(bf16[2,64,896]{2,1,0:T(8,128)(2,1)} %param.6) | copy-start | bytes 688132
  11.6 16.9 %copy-start.1 = (bf16[2,2048,896]{2,1,0:T(8,128)(2,1)S(1)}, bf16[2,2048,896]{2,1,0:T(8,128)(2,1)}, u32[]{:S(2)}) copy-start(bf16[2,2048,896]{2,1,0:T(8,128)(2,1)} %base_ref.3) | copy-start | bytes 22020100
  12.5 10.5 %collective-permute-start.7 = (bf16[4,2,8,2048]{3,2,1,0:T(8,128)(2,1)S(1)}, bf16[4,2,8,2048]{3,2,1,0:T(8,128)(2,1)S(1)}, u32[]{:S(2)}, u32[]{:S(2)}) collective-permute-start(bf16[4,2,8,2048]{3,2,1,0:T(8,128)(2,1)S(1)} %pad_maximum_fusion.2.refs_0_), channel_id=1, source_target_pairs={{0,2},{8,24},{16,18},{24,9},{1,3},{9,25},{17,19},{25,8},{2,4},{10,... | collective-permute-start | bytes 786440 | tf_op jit(solution)/shard_map/ppermute | solution.py:46
  14.2 10.2 %collective-permute-start.6 = (bf16[4,2,8,2048]{3,2,1,0:T(8,128)(2,1)S(1)}, bf16[4,2,8,2048]{3,2,1,0:T(8,128)(2,1)S(1)}, u32[]{:S(2)}, u32[]{:S(2)}) collective-permute-start(bf16[4,2,8,2048]{3,2,1,0:T(8,128)(2,1)S(1)} %pad_maximum_fusion.2.refs_0_), channel_id=1, source_target_pairs={{0,4},{8,9},{16,20},{24,25},{1,5},{9,8},{17,21},{25,24},{2,6},{10,... | collective-permute-start | bytes 786440 | tf_op jit(solution)/shard_map/ppermute | solution.py:46
  17.5 9.5 %collective-permute-start.5 = (bf16[4,2,8,2048]{3,2,1,0:T(8,128)(2,1)S(1)}, bf16[4,2,8,2048]{3,2,1,0:T(8,128)(2,1)S(1)}, u32[]{:S(2)}, u32[]{:S(2)}) collective-permute-start(bf16[4,2,8,2048]{3,2,1,0:T(8,128)(2,1)S(1)} %pad_maximum_fusion.2.refs_0_), channel_id=1, source_target_pairs={{0,6},{8,25},{16,22},{24,8},{1,7},{9,24},{17,23},{25,9},{2,0},{10,... | collective-permute-start | bytes 786440 | tf_op jit(solution)/shard_map/ppermute | solution.py:46
  18.2 8.7 %collective-permute-start.12 = (bf16[1,2,8,8,896]{4,3,2,1,0:T(8,128)(2,1)S(1)}, bf16[1,2,8,8,896]{4,3,2,1,0:T(8,128)(2,1)S(1)}, u32[]{:S(2)}, u32[]{:S(2)}) collective-permute-start(bf16[1,2,8,8,896]{4,3,2,1,0:T(8,128)(2,1)S(1)} %bitcast.4), channel_id=1, source_target_pairs={{0,64},{8,72},{16,80},{24,88},{1,65},{9,73},{17,81},{25,89},{2,66}... | collective-permute-start | bytes 688136 | tf_op jit(solution)/shard_map/ppermute | solution.py:46
  19.7 8.5 %collective-permute-start.8 = (bf16[4,2,8,2048]{3,2,1,0:T(8,128)(2,1)S(1)}, bf16[4,2,8,2048]{3,2,1,0:T(8,128)(2,1)S(1)}, u32[]{:S(2)}, u32[]{:S(2)}) collective-permute-start(bf16[4,2,8,2048]{3,2,1,0:T(8,128)(2,1)S(1)} %pad_maximum_fusion.2.refs_0_), channel_id=1, source_target_pairs={{0,8},{8,0},{16,24},{24,16},{1,9},{9,1},{17,25},{25,17},{2,10},{10... | collective-permute-start | bytes 786440 | tf_op jit(solution)/shard_map/ppermute | solution.py:46
  22.9 5.3 %collective-permute-start.11 = (bf16[4,2,8,2048]{3,2,1,0:T(8,128)(2,1)S(1)}, bf16[4,2,8,2048]{3,2,1,0:T(8,128)(2,1)S(1)}, u32[]{:S(2)}, u32[]{:S(2)}) collective-permute-start(bf16[4,2,8,2048]{3,2,1,0:T(8,128)(2,1)S(1)} %collective-permute-done.7.refs_3_), channel_id=1, source_target_pairs={{0,8},{8,0},{16,24},{24,16},{1,9},{9,1},{17,25},{25,17},{2,10},{10... | collective-permute-start | bytes 786440 | tf_op jit(solution)/shard_map/ppermute | solution.py:46
  24.3 3.9 %collective-permute-start.10 = (bf16[4,2,8,2048]{3,2,1,0:T(8,128)(2,1)S(1)}, bf16[4,2,8,2048]{3,2,1,0:T(8,128)(2,1)S(1)}, u32[]{:S(2)}, u32[]{:S(2)}) collective-permute-start(bf16[4,2,8,2048]{3,2,1,0:T(8,128)(2,1)S(1)} %collective-permute-done.6.refs_2_), channel_id=1, source_target_pairs={{0,8},{8,0},{16,24},{24,16},{1,9},{9,1},{17,25},{25,17},{2,10},{10... | collective-permute-start | bytes 786440 | tf_op jit(solution)/shard_map/ppermute | solution.py:46
  26.9 1.5 %collective-permute-start.9 = (bf16[4,2,8,2048]{3,2,1,0:T(8,128)(2,1)S(1)}, bf16[4,2,8,2048]{3,2,1,0:T(8,128)(2,1)S(1)}, u32[]{:S(2)}, u32[]{:S(2)}) collective-permute-start(bf16[4,2,8,2048]{3,2,1,0:T(8,128)(2,1)S(1)} %collective-permute-done.5.refs_1_), channel_id=1, source_target_pairs={{0,8},{8,0},{16,24},{24,16},{1,9},{9,1},{17,25},{25,17},{2,10},{10... | collective-permute-start | bytes 786440 | tf_op jit(solution)/shard_map/ppermute | solution.py:46

commit v3 on v2

--- a/solution.py
+++ b/solution.py
@@ -52,35 +52,52 @@
     ]
 
 
-def gather(base, adapter_down_stack, adapter_up_stack):
+def facing(x, second):
+    odd = x % 2
+    return (x + 3 + 2 * odd) % RING if second else x + 1 - 2 * odd
+
+
+def trade(piece, later):
+    pairs = [
+        (place_of(x, y, z, core), place_of(facing(x, core != later), y, z, core))
+        for x in range(RING)
+        for y in range(RING)
+        for z in range(RING)
+        for core in range(2)
+    ]
+    return lax.ppermute(piece, ALL_AXES, pairs)
+
+
+def gather(base, adapter_down_stack, adapter_up_stack, participant_weight):
     layers, ranks, cols = adapter_up_stack.shape
     up = adapter_up_stack.reshape(1, layers, ranks // 8, 8, cols)
-    near_up = jnp.concatenate([shift(up, dx=RING - 1), shift(up, dx=1)])
-    touched = touch(base)
+    near_up = jnp.concatenate([up, trade(up, False)])
+    far_up = trade(near_up, True)
     mine, *others = around(adapter_down_stack[None], "dz")
-    near_up, *others = gate([near_up] + others, [touched])
-    ring = jnp.concatenate([mine] + others)
-    own = around(ring, "dy")
-    far_up = shift(up, dx=2)
+    others = gate(others, [near_up, touch(base, [])])
+    ring = jnp.concatenate([mine, *others])
+    mine, *others = around(ring, "dy")
+    own = [mine, *others]
     other = [shift(piece, dcore=1) for piece in own]
-    b_groups = jnp.concatenate([up, near_up, far_up])
-    return own + other, b_groups
-
-
-def touch_kernel(base_ref, out_ref):
+    near_sorted, scale = sort_near(participant_weight, near_up)
+    return own + other, sort_far(far_up, near_sorted), scale
+
+
+def touch_kernel(base_ref, *refs):
+    out_ref = refs[-1]
     out_ref[...] = jnp.zeros(out_ref.shape, out_ref.dtype)
 
 
-def touch(base):
-    vmem = pl.BlockSpec(memory_space=pltpu.VMEM)
+def touch(base, after):
+    anywhere, vmem = pl.BlockSpec(memory_space=pl.ANY), pl.BlockSpec(memory_space=pltpu.VMEM)
     return pl.pallas_call(
         touch_kernel,
-        in_specs=[vmem],
+        in_specs=[vmem] + [anywhere] * len(after),
         out_specs=vmem,
         out_shape=jax.ShapeDtypeStruct((8, 128), jnp.float32),
         compiler_params=pltpu.CompilerParams(vmem_limit_bytes=VMEM_LIMIT),
         cost_estimate=pl.CostEstimate(flops=0, bytes_accessed=4 * base.size, transcendentals=0),
-    )(base)
+    )(base, *after)
 
 
 def gate(values, after):
@@ -97,9 +114,27 @@
     )(*values, *after)
 
 
-def sort_kernel(weight_ref, b_ref, out_ref, scale_ref):
+def place_blocks(b_ref, out_ref, far):
     row, col = lax.axis_index("row"), lax.axis_index("col")
     x, y, z, core = lax.axis_index("client"), col // 2, (col % 2) * 2 + row // 2, row % 2
+    early, late = facing(x, False), facing(x, True)
+    first_pair = jnp.where(core == 0, early, late)
+    last_pair = jnp.where(core == 0, late, early)
+    groups = (last_pair, lax.rem(x + 2, RING)) if far else (x, first_pair)
+    for i, group in enumerate(groups):
+        holder = lax.rem(group, 2)
+        for block in range(8):
+            dy = lax.rem(block // 2 - y + RING, RING)
+            dz = lax.rem(block % 2 * 2 + group // 2 - z + RING, RING)
+            first, second = jnp.where(holder == 0, dz, dy), jnp.where(holder == 0, dy, dz)
+            slot = (lax.rem(holder + core, 2) * RING + second) * RING + first
+            out_ref[:, slot] = b_ref[i, :, block]
+
+
+def near_kernel(weight_ref, near_ref, out_ref, scale_ref):
+    place_blocks(near_ref, out_ref, False)
+    row, col = lax.axis_index("row"), lax.axis_index("col")
+    y, z, core = col // 2, (col % 2) * 2 + row // 2, row % 2
     for dcore in range(2):
         holder = lax.rem(core + dcore, 2)
         for second in range(RING):
@@ -107,30 +142,43 @@
                 dy = jnp.where(holder == 0, second, first)
                 dz = jnp.where(holder == 0, first, second)
                 y_from, z_from = lax.rem(y + dy, RING), lax.rem(z + dz, RING)
-                group = lax.rem(z_from, 2) * 2 + holder
-                block = y_from * 2 + z_from // 2
-                slot = (dcore * RING + second) * RING + first
-                ahead = lax.rem(group - x + RING, RING)
-                out_ref[:, slot] = b_ref[jnp.where(ahead < 2, ahead, 5 - ahead), :, block]
-                scale_ref[slot] = jnp.full(
-                    scale_ref.shape[1:], weight_ref[group * 4 + block // 2], jnp.float32
+                client = (lax.rem(z_from, 2) * 2 + holder) * 4 + y_from
+                scale_ref[(dcore * RING + second) * RING + first] = jnp.full(
+                    scale_ref.shape[1:], weight_ref[client], jnp.float32
                 )
 
 
-def sort_up(participant_weight, b_groups):
-    _, layers, _, _, cols = b_groups.shape
+def sort_near(participant_weight, near_up):
+    _, layers, _, _, cols = near_up.shape
     vmem = pl.BlockSpec(memory_space=pltpu.VMEM)
     return pl.pallas_call(
-        sort_kernel,
+        near_kernel,
         in_specs=[pl.BlockSpec(memory_space=pltpu.SMEM), vmem],
         out_specs=[vmem, vmem],
         out_shape=[
-            jax.ShapeDtypeStruct((layers, BLOCKS, 8, cols), b_groups.dtype),
+            jax.ShapeDtypeStruct((layers, BLOCKS, 8, cols), near_up.dtype),
             jax.ShapeDtypeStruct((BLOCKS, 8, 128), jnp.float32),
         ],
         compiler_params=pltpu.CompilerParams(vmem_limit_bytes=VMEM_LIMIT),
-        cost_estimate=pl.CostEstimate(flops=0, bytes_accessed=4 * b_groups.size, transcendentals=0),
-    )(participant_weight, b_groups)
+        cost_estimate=pl.CostEstimate(flops=0, bytes_accessed=4 * near_up.size, transcendentals=0),
+    )(participant_weight, near_up)
+
+
+def far_kernel(far_ref, _, out_ref):
+    place_blocks(far_ref, out_ref, True)
+
+
+def sort_far(far_up, near_sorted):
+    vmem = pl.BlockSpec(memory_space=pltpu.VMEM)
+    return pl.pallas_call(
+        far_kernel,
+        in_specs=[vmem, vmem],
+        out_specs=vmem,
+        out_shape=jax.ShapeDtypeStruct(near_sorted.shape, near_sorted.dtype),
+        input_output_aliases={1: 0},
+        compiler_params=pltpu.CompilerParams(vmem_limit_bytes=VMEM_LIMIT),
+        cost_estimate=pl.CostEstimate(flops=0, bytes_accessed=4 * far_up.size, transcendentals=0),
+    )(far_up, near_sorted)
 
 
 def merge_kernel(base_ref, *refs):
@@ -145,7 +193,7 @@
     for layer in range(layers):
         right = b_ref[layer].reshape(ranks, cols)
 
-        @pl.loop(0, rows // tall, unroll=4)
+        @pl.loop(0, rows // tall, unroll=8)
         def _(i):
             span = pl.ds(pl.multiple_of(i * tall, tall), tall)
             left = jnp.concatenate(
@@ -178,33 +226,43 @@
     )(base, *a_pieces, b_sorted, scale)
 
 
-def settle_kernel(in_ref, out_ref, sems):
-    parts, layers, _, cols = in_ref.shape
-    copies = [
-        pltpu.make_async_copy(
-            in_ref.at[spot_of(y, z, core), layer],
-            out_ref.at[layer, :, pl.ds(place_of(0, y, z, core) * cols, cols)],
-            sems.at[spot_of(y, z, core), layer],
-        )
-        for y in range(RING)
-        for z in range(RING)
-        for core in range(2)
-        for layer in range(layers)
-    ]
-    for copy in copies:
-        copy.start()
+def settle_kernel(in_ref, out_ref, lines, sems):
+    _, layers, part_rows, cols = in_ref.shape
+    tall = lines.shape[1]
+    copies = []
+    for layer in range(layers):
+        for first in range(0, part_rows, tall):
+            slot = len(copies)
+            for y in range(RING):
+                for z in range(RING):
+                    for core in range(2):
+                        left = place_of(0, y, z, core) * cols
+                        lines[slot, :, left : left + cols] = in_ref[
+                            spot_of(y, z, core), layer, first : first + tall
+                        ]
+            copies.append(
+                pltpu.make_async_copy(
+                    lines.at[slot], out_ref.at[layer, pl.ds(first, tall)], sems.at[slot]
+                )
+            )
+            copies[-1].start()
     for copy in copies:
         copy.wait()
 
 
 def settle(received):
     parts, layers, part_rows, cols = received.shape
+    tall = 16
+    slots = layers * part_rows // tall
     return pl.pallas_call(
         settle_kernel,
         in_specs=[pl.BlockSpec(memory_space=pltpu.VMEM)],
         out_specs=pl.BlockSpec(memory_space=pl.ANY),
         out_shape=jax.ShapeDtypeStruct((layers, part_rows, parts * cols), jnp.bfloat16),
-        scratch_shapes=[pltpu.SemaphoreType.DMA((parts, layers))],
+        scratch_shapes=[
+            pltpu.VMEM((slots, tall, parts * cols), jnp.bfloat16),
+            pltpu.SemaphoreType.DMA((slots,)),
+        ],
         compiler_params=pltpu.CompilerParams(vmem_limit_bytes=VMEM_LIMIT),
         cost_estimate=pl.CostEstimate(flops=0, bytes_accessed=4 * received.size, transcendentals=0),
     )(received)
@@ -212,8 +270,9 @@
 
 def local(frozen_up_weight, adapter_down_stack, adapter_up_stack, participant_weight):
     parts = lax.axis_size(TILE_AXES)
-    a_pieces, b_groups = gather(frozen_up_weight, adapter_down_stack, adapter_up_stack)
-    b_sorted, scale = sort_up(participant_weight, b_groups)
+    a_pieces, b_sorted, scale = gather(
+        frozen_up_weight, adapter_down_stack, adapter_up_stack, participant_weight
+    )
     merged = merge(frozen_up_weight, a_pieces, b_sorted, scale, parts)
     return settle(exchange(merged))
 

time: 125 us -> 123 us (0.984)
  starting transfers between devices: 21.6 us -> 18.5 us
  waiting for transfers between devices: 1.63 us -> 3.14 us
    ppermute x13 -> x10, starting transfers between devices: 21.6 us -> 15.2 us  [shift(): return lax.ppermute(piece, ALL_AXES, pairs)]
    ppermute x0 -> x2, starting transfers between devices: none -> 3.31 us  [trade(): return lax.ppermute(piece, ALL_AXES, pairs)]
    ppermute x13 -> x10, waiting for transfers between devices: 1.63 us -> 3.14 us  [shift(): return lax.ppermute(piece, ALL_AXES, pairs)]
    unnamed x10 -> x8, local copies, waits for them, and re-layouts: 3.8 us -> 3.09 us
  transfers between devices with their start and end apart: 13 -> 12, of which waited for: 2 -> 3; matrix products, arithmetic and copies ran while one was open for 0% -> 1% of each run, Pallas kernels for 1% -> 1%
where the time goes in v3:
time: 123 us
  blocking collectives  89.9 us (73%)
  starting transfers between devices  18.5 us (15%)
  Pallas kernels  6.81 us (6%)
  waiting for transfers between devices  3.14 us (3%)
  local copies, waits for them, and re-layouts  3.09 us (3%)
    all_to_all x1, blocking collectives, exchange(): lax.all_to_all(pieces, TILE_AXES, split_axis=0, concat_axis=0, axis_index...  89.9 us
    ppermute x10, starting transfers between devices, shift(): return lax.ppermute(piece, ALL_AXES, pairs)  15.2 us
    ppermute x2, starting transfers between devices, trade(): return lax.ppermute(piece, ALL_AXES, pairs)  3.31 us
    ppermute x10, waiting for transfers between devices, shift(): return lax.ppermute(piece, ALL_AXES, pairs)  3.14 us
    pallas_call x1, Pallas kernels, settle(): pl.pallas_call(settle_kernel, in_specs=[pl.BlockSpec(memory_space=pltpu.V...  3.12 us
    unnamed x8, local copies, waits for them, and re-layouts  3.09 us
    pallas_call x1, Pallas kernels, merge(): pl.pallas_call(merge_kernel, in_specs=[vmem] * (len(a_pieces) + 3), out_s...  2.67 us
  transfers between devices with their start and end apart: 12, of which 3 were waited for; matrix products, arithmetic and copies ran while one was open for 1% of the time, Pallas kernels for 1%

profile of v3, /device:TPU:1, one launch (start us, length us, event | category | flops | bytes accessed | tf_op | source)
XLA Modules:
  0.0 122.8 jit_solution(6839965809743864899)
XLA Ops:
  0.0 0.0 copy-start.2
  0.0 3.3 %collective-permute-start.3 = (bf16[1,2,8,8,896]{4,3,2,1,0:T(8,128)(2,1)}, bf16[1,2,8,8,896]{4,3,2,1,0:T(8,128)(2,1)S(1)}, u32[]{:S(2)}, u32[]{:S(2)}) collective-permute-start(bf16[1,2,8,8,896]{4,3,2,1,0:T(8,128)(2,1)} %bitcast.2), channel_id=1, source_target_pairs={{0,32},{8,104},{16,48},{24,120},{1,33},{9,105},{17,49},{25,121},{2... | collective-permute-start | bytes 688136 | tf_op jit(solution)/shard_map/ppermute | solution.py:68
  3.3 1.3 %collective-permute-start.2 = (bf16[1,2,8,2048]{3,2,1,0:T(8,128)(2,1)}, bf16[1,2,8,2048]{3,2,1,0:T(8,128)(2,1)S(1)}, u32[]{:S(2)}, u32[]{:S(2)}) collective-permute-start(bf16[1,2,8,2048]{3,2,1,0:T(8,128)(2,1)} %bitcast.4), channel_id=1, source_target_pairs={{0,16},{8,10},{16,1},{24,26},{1,17},{9,11},{17,0},{25,27},{2,18},{... | collective-permute-start | bytes 196616 | tf_op jit(solution)/shard_map/ppermute | solution.py:46
  4.6 2.6 %collective-permute-start.1 = (bf16[1,2,8,2048]{3,2,1,0:T(8,128)(2,1)}, bf16[1,2,8,2048]{3,2,1,0:T(8,128)(2,1)S(1)}, u32[]{:S(2)}, u32[]{:S(2)}) collective-permute-start(bf16[1,2,8,2048]{3,2,1,0:T(8,128)(2,1)} %bitcast.5), channel_id=1, source_target_pairs={{0,1},{8,12},{16,17},{24,28},{1,0},{9,13},{17,16},{25,29},{2,3},{1... | collective-permute-start | bytes 196616 | tf_op jit(solution)/shard_map/ppermute | solution.py:46
  7.2 1.1 collective-permute-start
  8.3 0.0 copy-start
  8.3 3.1 %copy-done = bf16[2,2048,896]{2,1,0:T(8,128)(2,1)S(1)} copy-done((bf16[2,2048,896]{2,1,0:T(8,128)(2,1)S(1)}, bf16[2,2048,896]{2,1,0:T(8,128)(2,1)}, u32[]{:S(2)}) %copy-start) | copy-done | bytes 7340056
  11.4 0.0 copy-start.3
  11.4 0.0 copy-start.1
  11.4 0.0 collective-permute-done.3
  11.4 1.1 pad_maximum_fusion.refs_3_.near_ref
  12.5 0.0 collective-permute-done.2.refs_2_
  12.5 0.0 collective-permute-done.1.refs_1_
  12.6 0.0 collective-permute-done.refs_0_
  12.6 0.0 copy-done.3
  12.6 1.7 %collective-permute-start.6 = (bf16[4,2,8,2048]{3,2,1,0:T(8,128)(2,1)S(1)}, bf16[4,2,8,2048]{3,2,1,0:T(8,128)(2,1)S(1)}, u32[]{:S(2)}, u32[]{:S(2)}) collective-permute-start(bf16[4,2,8,2048]{3,2,1,0:T(8,128)(2,1)S(1)} %pad_maximum_fusion.1.refs_0_), channel_id=1, source_target_pairs={{0,2},{8,24},{16,18},{24,9},{1,3},{9,25},{17,19},{25,8},{2,4},{10,... | collective-permute-start | bytes 786440 | tf_op jit(solution)/shard_map/ppermute | solution.py:46
  14.3 3.3 %collective-permute-start.5 = (bf16[4,2,8,2048]{3,2,1,0:T(8,128)(2,1)S(1)}, bf16[4,2,8,2048]{3,2,1,0:T(8,128)(2,1)S(1)}, u32[]{:S(2)}, u32[]{:S(2)}) collective-permute-start(bf16[4,2,8,2048]{3,2,1,0:T(8,128)(2,1)S(1)} %pad_maximum_fusion.1.refs_0_), channel_id=1, source_target_pairs={{0,4},{8,9},{16,20},{24,25},{1,5},{9,8},{17,21},{25,24},{2,6},{10,... | collective-permute-start | bytes 786440 | tf_op jit(solution)/shard_map/ppermute | solution.py:46
  17.6 0.7 collective-permute-start.4
  18.4 0.0 collective-permute-start.11
  18.4 3.5 %collective-permute-start.7 = (bf16[4,2,8,2048]{3,2,1,0:T(8,128)(2,1)S(1)}, bf16[4,2,8,2048]{3,2,1,0:T(8,128)(2,1)S(1)}, u32[]{:S(2)}, u32[]{:S(2)}) collective-permute-start(bf16[4,2,8,2048]{3,2,1,0:T(8,128)(2,1)S(1)} %pad_maximum_fusion.1.refs_0_), channel_id=1, source_target_pairs={{0,8},{8,0},{16,24},{24,16},{1,9},{9,1},{17,25},{25,17},{2,10},{10... | collective-permute-start | bytes 786440 | tf_op jit(solution)/shard_map/ppermute | solution.py:46
  21.8 0.0 collective-permute-done.6.refs_3_
  21.8 0.0 collective-permute-start.10
  21.8 2.7 %collective-permute-done.5.refs_2_ = bf16[4,2,8,2048]{3,2,1,0:T(8,128)(2,1)S(1)} collective-permute-done((bf16[4,2,8,2048]{3,2,1,0:T(8,128)(2,1)S(1)}, bf16[4,2,8,2048]{3,2,1,0:T(8,128)(2,1)S(1)}, u32[]{:S(2)}, u32[]{:S(2)}) %collective-permute-start.5) | collective-permute-done | bytes 262176 | tf_op jit(solution)/shard_map/ppermute | solution.py:46
  24.5 1.0 collective-permute-start.9
  25.5 0.0 collective-permute-done.4.refs_1_
  25.5 0.0 collective-permute-start.8
  25.6 0.0 copy-done.2
  25.6 0.9 shard_map.48
  26.5 0.0 collective-permute-done.11.far_ref
  26.5 0.1 shard_map.49.refs_8_
  26.6 0.0 collective-permute-done.7.refs_4_
  26.6 0.0 collective-permute-done.10.refs_7_
  26.6 0.1 collective-permute-done.9.refs_6_
  26.7 0.4 collective-permute-done.8.refs_5_
  27.1 0.0 copy-done.1
  27.1 2.7 %shard_map.50 = bf16[32,2,64,896]{3,2,1,0:T(8,128)(2,1)S(1)} custom-call(bf16[2,2048,896]{2,1,0:T(8,128)(2,1)S(1)} %copy-done.1, bf16[4,2,8,2048]{3,2,1,0:T(8,128)(2,1)S(1)} %pad_maximum_fusion.1.refs_0_, bf16[4,2,8,2048]{3,2,1,0:T(8,128)(2,1)S(1)} %collective-permute-done.4.refs_1_, bf16[4,2,8,2048]{3,2,1,0:T(8,128)(2,1)S(1)} %collective-permute-done.5.refs_2_, ...), custom_call_target="tpu_custom_call" | custom-call | flops 1879048192 | bytes 14680064 | tf_op jit(solution)/shard_map/pallas_call | solution.py:217
  29.8 89.9 %all_to_all.5.in_ref = bf16[32,2,64,896]{3,2,1,0:T(8,128)(2,1)S(1)} all-to-all(bf16[32,2,64,896]{3,2,1,0:T(8,128)(2,1)S(1)} %shard_map.50), channel_id=1, replica_groups={{0,8,16,24,1,9,17,25,4,12,20,28,5,13,21,29,2,10,18,26,3,11,19,27,6,14,2..., dimensions={0} | all-to-all | bytes 14680064 | tf_op jit(solution)/shard_map/all_to_all | solution.py:30
  119.7 3.1 %shard_map.51 = bf16[2,64,28672]{2,1,0:T(8,128)(2,1)} custom-call(bf16[32,2,64,896]{3,2,1,0:T(8,128)(2,1)S(1)} %all_to_all.5.in_ref), custom_call_target="tpu_custom_call" | custom-call | bytes 14680064 | tf_op jit(solution)/shard_map/pallas_call | solution.py:257
  (3 shorter events, 0.0 us)
Async XLA Ops:
  0.0 25.6 %copy-start.2 = (f32[16]{0:T(128)S(1)}, f32[16]{0:T(128)}, u32[]{:S(2)}) copy-start(f32[16]{0:T(128)} %weight_ref.1) | copy-start | bytes 196
  0.0 11.4 %collective-permute-start.3 = (bf16[1,2,8,8,896]{4,3,2,1,0:T(8,128)(2,1)}, bf16[1,2,8,8,896]{4,3,2,1,0:T(8,128)(2,1)S(1)}, u32[]{:S(2)}, u32[]{:S(2)}) collective-permute-start(bf16[1,2,8,8,896]{4,3,2,1,0:T(8,128)(2,1)} %bitcast.2), channel_id=1, source_target_pairs={{0,32},{8,104},{16,48},{24,120},{1,33},{9,105},{17,49},{25,121},{2... | collective-permute-start | bytes 688136 | tf_op jit(solution)/shard_map/ppermute | solution.py:68
  3.3 9.2 %collective-permute-start.2 = (bf16[1,2,8,2048]{3,2,1,0:T(8,128)(2,1)}, bf16[1,2,8,2048]{3,2,1,0:T(8,128)(2,1)S(1)}, u32[]{:S(2)}, u32[]{:S(2)}) collective-permute-start(bf16[1,2,8,2048]{3,2,1,0:T(8,128)(2,1)} %bitcast.4), channel_id=1, source_target_pairs={{0,16},{8,10},{16,1},{24,26},{1,17},{9,11},{17,0},{25,27},{2,18},{... | collective-permute-start | bytes 196616 | tf_op jit(solution)/shard_map/ppermute | solution.py:46
  4.6 7.9 %collective-permute-start.1 = (bf16[1,2,8,2048]{3,2,1,0:T(8,128)(2,1)}, bf16[1,2,8,2048]{3,2,1,0:T(8,128)(2,1)S(1)}, u32[]{:S(2)}, u32[]{:S(2)}) collective-permute-start(bf16[1,2,8,2048]{3,2,1,0:T(8,128)(2,1)} %bitcast.5), channel_id=1, source_target_pairs={{0,1},{8,12},{16,17},{24,28},{1,0},{9,13},{17,16},{25,29},{2,3},{1... | collective-permute-start | bytes 196616 | tf_op jit(solution)/shard_map/ppermute | solution.py:46
  7.2 5.3 %collective-permute-start = (bf16[1,2,8,2048]{3,2,1,0:T(8,128)(2,1)}, bf16[1,2,8,2048]{3,2,1,0:T(8,128)(2,1)S(1)}, u32[]{:S(2)}, u32[]{:S(2)}) collective-permute-start(bf16[1,2,8,2048]{3,2,1,0:T(8,128)(2,1)} %bitcast.6), channel_id=1, source_target_pairs={{0,17},{8,14},{16,0},{24,30},{1,16},{9,15},{17,1},{25,31},{2,19},{... | collective-permute-start | bytes 196616 | tf_op jit(solution)/shard_map/ppermute | solution.py:46
  8.3 3.1 %copy-start = (bf16[2,2048,896]{2,1,0:T(8,128)(2,1)S(1)}, bf16[2,2048,896]{2,1,0:T(8,128)(2,1)}, u32[]{:S(2)}) copy-start(bf16[2,2048,896]{2,1,0:T(8,128)(2,1)} %base_ref.3) | copy-start | bytes 22020100
  11.4 1.2 copy-start.3
  11.4 15.7 %copy-start.1 = (bf16[2,2048,896]{2,1,0:T(8,128)(2,1)S(1)}, bf16[2,2048,896]{2,1,0:T(8,128)(2,1)}, u32[]{:S(2)}) copy-start(bf16[2,2048,896]{2,1,0:T(8,128)(2,1)} %base_ref.3) | copy-start | bytes 22020100
  12.6 9.2 %collective-permute-start.6 = (bf16[4,2,8,2048]{3,2,1,0:T(8,128)(2,1)S(1)}, bf16[4,2,8,2048]{3,2,1,0:T(8,128)(2,1)S(1)}, u32[]{:S(2)}, u32[]{:S(2)}) collective-permute-start(bf16[4,2,8,2048]{3,2,1,0:T(8,128)(2,1)S(1)} %pad_maximum_fusion.1.refs_0_), channel_id=1, source_target_pairs={{0,2},{8,24},{16,18},{24,9},{1,3},{9,25},{17,19},{25,8},{2,4},{10,... | collective-permute-start | bytes 786440 | tf_op jit(solution)/shard_map/ppermute | solution.py:46
  14.3 10.2 %collective-permute-start.5 = (bf16[4,2,8,2048]{3,2,1,0:T(8,128)(2,1)S(1)}, bf16[4,2,8,2048]{3,2,1,0:T(8,128)(2,1)S(1)}, u32[]{:S(2)}, u32[]{:S(2)}) collective-permute-start(bf16[4,2,8,2048]{3,2,1,0:T(8,128)(2,1)S(1)} %pad_maximum_fusion.1.refs_0_), channel_id=1, source_target_pairs={{0,4},{8,9},{16,20},{24,25},{1,5},{9,8},{17,21},{25,24},{2,6},{10,... | collective-permute-start | bytes 786440 | tf_op jit(solution)/shard_map/ppermute | solution.py:46
  17.6 7.9 %collective-permute-start.4 = (bf16[4,2,8,2048]{3,2,1,0:T(8,128)(2,1)S(1)}, bf16[4,2,8,2048]{3,2,1,0:T(8,128)(2,1)S(1)}, u32[]{:S(2)}, u32[]{:S(2)}) collective-permute-start(bf16[4,2,8,2048]{3,2,1,0:T(8,128)(2,1)S(1)} %pad_maximum_fusion.1.refs_0_), channel_id=1, source_target_pairs={{0,6},{8,25},{16,22},{24,8},{1,7},{9,24},{17,23},{25,9},{2,0},{10,... | collective-permute-start | bytes 786440 | tf_op jit(solution)/shard_map/ppermute | solution.py:46
  18.4 8.1 %collective-permute-start.11 = (bf16[2,2,8,8,896]{4,3,2,1,0:T(8,128)(2,1)S(1)}, bf16[2,2,8,8,896]{4,3,2,1,0:T(8,128)(2,1)S(1)}, u32[]{:S(2)}, u32[]{:S(2)}) collective-permute-start(bf16[2,2,8,8,896]{4,3,2,1,0:T(8,128)(2,1)S(1)} %pad_maximum_fusion.refs_3_.near_ref), channel_id=1, source_target_pairs={{0,96},{8,40},{16,112},{24,56},{1,97},{9,41},{17,113},{25,57},{2,9... | collective-permute-start | bytes 1376264 | tf_op jit(solution)/shard_map/ppermute | solution.py:68
  18.4 8.2 %collective-permute-start.7 = (bf16[4,2,8,2048]{3,2,1,0:T(8,128)(2,1)S(1)}, bf16[4,2,8,2048]{3,2,1,0:T(8,128)(2,1)S(1)}, u32[]{:S(2)}, u32[]{:S(2)}) collective-permute-start(bf16[4,2,8,2048]{3,2,1,0:T(8,128)(2,1)S(1)} %pad_maximum_fusion.1.refs_0_), channel_id=1, source_target_pairs={{0,8},{8,0},{16,24},{24,16},{1,9},{9,1},{17,25},{25,17},{2,10},{10... | collective-permute-start | bytes 786440 | tf_op jit(solution)/shard_map/ppermute | solution.py:46
  21.8 4.8 %collective-permute-start.10 = (bf16[4,2,8,2048]{3,2,1,0:T(8,128)(2,1)S(1)}, bf16[4,2,8,2048]{3,2,1,0:T(8,128)(2,1)S(1)}, u32[]{:S(2)}, u32[]{:S(2)}) collective-permute-start(bf16[4,2,8,2048]{3,2,1,0:T(8,128)(2,1)S(1)} %collective-permute-done.6.refs_3_), channel_id=1, source_target_pairs={{0,8},{8,0},{16,24},{24,16},{1,9},{9,1},{17,25},{25,17},{2,10},{10... | collective-permute-start | bytes 786440 | tf_op jit(solution)/shard_map/ppermute | solution.py:46
  24.5 2.2 %collective-permute-start.9 = (bf16[4,2,8,2048]{3,2,1,0:T(8,128)(2,1)S(1)}, bf16[4,2,8,2048]{3,2,1,0:T(8,128)(2,1)S(1)}, u32[]{:S(2)}, u32[]{:S(2)}) collective-permute-start(bf16[4,2,8,2048]{3,2,1,0:T(8,128)(2,1)S(1)} %collective-permute-done.5.refs_2_), channel_id=1, source_target_pairs={{0,8},{8,0},{16,24},{24,16},{1,9},{9,1},{17,25},{25,17},{2,10},{10... | collective-permute-start | bytes 786440 | tf_op jit(solution)/shard_map/ppermute | solution.py:46
  25.5 1.5 %collective-permute-start.8 = (bf16[4,2,8,2048]{3,2,1,0:T(8,128)(2,1)S(1)}, bf16[4,2,8,2048]{3,2,1,0:T(8,128)(2,1)S(1)}, u32[]{:S(2)}, u32[]{:S(2)}) collective-permute-start(bf16[4,2,8,2048]{3,2,1,0:T(8,128)(2,1)S(1)} %collective-permute-done.4.refs_1_), channel_id=1, source_target_pairs={{0,8},{8,0},{16,24},{24,16},{1,9},{9,1},{17,25},{25,17},{2,10},{10... | collective-permute-start | bytes 786440 | tf_op jit(solution)/shard_map/ppermute | solution.py:46

commit v4 on v3

--- a/solution.py
+++ b/solution.py
@@ -18,7 +18,7 @@
 
 
 def spot_of(y, z, core):
-    return (y % 2) * 16 + (y // 2) * 8 + (z // 2) * 4 + (z % 2) * 2 + core
+    return z * 8 + (y % 2) * 4 + core * 2 + y // 2
 
 
 def exchange(pieces):
@@ -73,14 +73,35 @@
     up = adapter_up_stack.reshape(1, layers, ranks // 8, 8, cols)
     near_up = jnp.concatenate([up, trade(up, False)])
     far_up = trade(near_up, True)
-    mine, *others = around(adapter_down_stack[None], "dz")
-    others = gate(others, [near_up, touch(base, [])])
-    ring = jnp.concatenate([mine, *others])
+    (here,) = stage([adapter_down_stack[None]])
+    _, *others = around(adapter_down_stack[None], "dz")
+    ring = jnp.concatenate([here, *others])
     mine, *others = around(ring, "dy")
+    near_sorted, scale = sort_near(participant_weight, near_up)
+    b_sorted = sort_far(far_up, near_sorted)
+    touched = touch(base, [])
+    others = [gate([piece], [touched, far_up])[0] for piece in others]
     own = [mine, *others]
     other = [shift(piece, dcore=1) for piece in own]
-    near_sorted, scale = sort_near(participant_weight, near_up)
-    return own + other, sort_far(far_up, near_sorted), scale
+    return own + other, b_sorted, scale
+
+
+def stage_kernel(*refs):
+    half = len(refs) // 2
+    for in_ref, out_ref in zip(refs[:half], refs[half:]):
+        out_ref[...] = in_ref[...]
+
+
+def stage(arrays):
+    vmem = pl.BlockSpec(memory_space=pltpu.VMEM)
+    return pl.pallas_call(
+        stage_kernel,
+        in_specs=[vmem] * len(arrays),
+        out_specs=[vmem] * len(arrays),
+        out_shape=[jax.ShapeDtypeStruct(a.shape, a.dtype) for a in arrays],
+        compiler_params=pltpu.CompilerParams(vmem_limit_bytes=VMEM_LIMIT),
+        cost_estimate=pl.CostEstimate(flops=0, bytes_accessed=1 << 20, transcendentals=0),
+    )(*arrays)
 
 
 def touch_kernel(base_ref, *refs):

time: 123 us -> 122 us (level)
  starting transfers between devices: 18.5 us -> 21.8 us
  blocking collectives: 89.9 us -> 87.1 us
  waiting for transfers between devices: 3.14 us -> 0.68 us
    ppermute x10, starting transfers between devices: 15.2 us -> 18.4 us  [shift(): return lax.ppermute(piece, ALL_AXES, pairs)]
    all_to_all x1, blocking collectives: 89.9 us -> 87.1 us  [exchange(): lax.all_to_all(pieces, TILE_AXES, split_axis=0, concat_axis=0, axis_index...]
    ppermute x10, waiting for transfers between devices: 3.14 us -> 0.68 us  [shift(): return lax.ppermute(piece, ALL_AXES, pairs)]
  transfers between devices with their start and end apart: 12 -> 12, of which waited for: 3 -> 2; matrix products, arithmetic and copies ran while one was open for 1% -> 1% of each run, Pallas kernels for 1% -> 1%
where the time goes in v4:
time: 122 us; the launch traced here: 121 us
  blocking collectives  87.1 us (71%)
  starting transfers between devices  21.8 us (18%)
  Pallas kernels  6.82 us (6%)
  local copies, waits for them, and re-layouts  3.96 us (3%)
    all_to_all x1, blocking collectives, exchange(): lax.all_to_all(pieces, TILE_AXES, split_axis=0, concat_axis=0, axis_index...  87.1 us
    ppermute x10, starting transfers between devices, shift(): return lax.ppermute(piece, ALL_AXES, pairs)  18.4 us
    unnamed x8, local copies, waits for them, and re-layouts  3.96 us
    ppermute x2, starting transfers between devices, trade(): return lax.ppermute(piece, ALL_AXES, pairs)  3.39 us
    pallas_call x1, Pallas kernels, settle(): pl.pallas_call(settle_kernel, in_specs=[pl.BlockSpec(memory_space=pltpu.V...  3.12 us
    pallas_call x1, Pallas kernels, merge(): pl.pallas_call(merge_kernel, in_specs=[vmem] * (len(a_pieces) + 3), out_s...  2.67 us
  transfers between devices with their start and end apart: 12, of which 2 were waited for; matrix products, arithmetic and copies ran while one was open for 1% of the time, Pallas kernels for 1%

profile of v4, /device:TPU:1, one launch (start us, length us, event | category | flops | bytes accessed | tf_op | source)
XLA Modules:
  0.0 121.5 jit_solution(5280885990971899784)
XLA Ops:
  0.0 0.0 copy-start.3
  0.0 3.3 %collective-permute-start.4 = (bf16[1,2,8,8,896]{4,3,2,1,0:T(8,128)(2,1)}, bf16[1,2,8,8,896]{4,3,2,1,0:T(8,128)(2,1)S(1)}, u32[]{:S(2)}, u32[]{:S(2)}) collective-permute-start(bf16[1,2,8,8,896]{4,3,2,1,0:T(8,128)(2,1)} %bitcast.6), channel_id=1, source_target_pairs={{0,32},{8,104},{16,48},{24,120},{1,33},{9,105},{17,49},{25,121},{2... | collective-permute-start | bytes 688136 | tf_op jit(solution)/shard_map/ppermute | solution.py:68
  3.3 1.3 %collective-permute-start.2 = (bf16[1,2,8,2048]{3,2,1,0:T(8,128)(2,1)}, bf16[1,2,8,2048]{3,2,1,0:T(8,128)(2,1)S(1)}, u32[]{:S(2)}, u32[]{:S(2)}) collective-permute-start(bf16[1,2,8,2048]{3,2,1,0:T(8,128)(2,1)} %bitcast.2), channel_id=1, source_target_pairs={{0,16},{8,10},{16,1},{24,26},{1,17},{9,11},{17,0},{25,27},{2,18},{... | collective-permute-start | bytes 196616 | tf_op jit(solution)/shard_map/ppermute | solution.py:46
  4.6 2.6 %collective-permute-start.1 = (bf16[1,2,8,2048]{3,2,1,0:T(8,128)(2,1)}, bf16[1,2,8,2048]{3,2,1,0:T(8,128)(2,1)S(1)}, u32[]{:S(2)}, u32[]{:S(2)}) collective-permute-start(bf16[1,2,8,2048]{3,2,1,0:T(8,128)(2,1)} %bitcast.3), channel_id=1, source_target_pairs={{0,1},{8,12},{16,17},{24,28},{1,0},{9,13},{17,16},{25,29},{2,3},{1... | collective-permute-start | bytes 196616 | tf_op jit(solution)/shard_map/ppermute | solution.py:46
  7.2 1.1 collective-permute-start
  8.3 0.0 copy-start.2
  8.3 0.9 copy-done.2
  9.2 0.0 collective-permute-done.4
  9.2 1.0 pad_maximum_fusion.near_ref
  10.2 0.1 collective-permute-start.5
  10.3 0.0 collective-permute-done.2
  10.3 0.0 collective-permute-done.1
  10.3 0.6 collective-permute-done
  10.9 3.7 %collective-permute-start.3 = (bf16[4,2,8,2048]{3,2,1,0:T(8,128)(2,1)S(1)}, bf16[4,2,8,2048]{3,2,1,0:T(8,128)(2,1)S(1)}, u32[]{:S(2)}, u32[]{:S(2)}) collective-permute-start(bf16[4,2,8,2048]{3,2,1,0:T(8,128)(2,1)S(1)} %pad_maximum_fusion.1.refs_0_), channel_id=1, source_target_pairs={{0,6},{8,25},{16,22},{24,8},{1,7},{9,24},{17,23},{25,9},{2,0},{10,... | collective-permute-start | bytes 786440 | tf_op jit(solution)/shard_map/ppermute | solution.py:46
  14.6 0.0 collective-permute-start.6
  14.6 0.7 collective-permute-start.7
  15.3 0.0 copy-start
  15.3 3.1 %copy-done = bf16[2,2048,896]{2,1,0:T(8,128)(2,1)S(1)} copy-done((bf16[2,2048,896]{2,1,0:T(8,128)(2,1)S(1)}, bf16[2,2048,896]{2,1,0:T(8,128)(2,1)}, u32[]{:S(2)}) %copy-start) | copy-done | bytes 7340056
  18.4 0.0 copy-start.1
  18.4 3.0 %collective-permute-start.8 = (bf16[4,2,8,2048]{3,2,1,0:T(8,128)(2,1)S(1)}, bf16[4,2,8,2048]{3,2,1,0:T(8,128)(2,1)S(1)}, u32[]{:S(2)}, u32[]{:S(2)}) collective-permute-start(bf16[4,2,8,2048]{3,2,1,0:T(8,128)(2,1)S(1)} %pad_maximum_fusion.1.refs_0_), channel_id=1, source_target_pairs={{0,8},{8,0},{16,24},{24,16},{1,9},{9,1},{17,25},{25,17},{2,10},{10... | collective-permute-start | bytes 786440 | tf_op jit(solution)/shard_map/ppermute | solution.py:46
  21.4 0.0 collective-permute-done.3.refs_0_
  21.4 0.0 collective-permute-done.5.refs_2_.far_ref
  21.4 2.0 %collective-permute-start.9 = (bf16[4,2,8,2048]{3,2,1,0:T(8,128)(2,1)S(1)}, bf16[4,2,8,2048]{3,2,1,0:T(8,128)(2,1)S(1)}, u32[]{:S(2)}, u32[]{:S(2)}) collective-permute-start(bf16[4,2,8,2048]{3,2,1,0:T(8,128)(2,1)S(1)} %shard_map.48.refs_1_), channel_id=1, source_target_pairs={{0,8},{8,0},{16,24},{24,16},{1,9},{9,1},{17,25},{25,17},{2,10},{10... | collective-permute-start | bytes 786440 | tf_op jit(solution)/shard_map/ppermute | solution.py:46
  23.4 0.0 collective-permute-done.6.refs_0_
  23.4 1.3 %collective-permute-start.10 = (bf16[4,2,8,2048]{3,2,1,0:T(8,128)(2,1)S(1)}, bf16[4,2,8,2048]{3,2,1,0:T(8,128)(2,1)S(1)}, u32[]{:S(2)}, u32[]{:S(2)}) collective-permute-start(bf16[4,2,8,2048]{3,2,1,0:T(8,128)(2,1)S(1)} %shard_map.49.refs_2_), channel_id=1, source_target_pairs={{0,8},{8,0},{16,24},{24,16},{1,9},{9,1},{17,25},{25,17},{2,10},{10... | collective-permute-start | bytes 786440 | tf_op jit(solution)/shard_map/ppermute | solution.py:46
  24.7 0.0 collective-permute-done.7.refs_0_
  24.7 2.7 %collective-permute-start.11 = (bf16[4,2,8,2048]{3,2,1,0:T(8,128)(2,1)S(1)}, bf16[4,2,8,2048]{3,2,1,0:T(8,128)(2,1)S(1)}, u32[]{:S(2)}, u32[]{:S(2)}) collective-permute-start(bf16[4,2,8,2048]{3,2,1,0:T(8,128)(2,1)S(1)} %shard_map.50.refs_3_), channel_id=1, source_target_pairs={{0,8},{8,0},{16,24},{24,16},{1,9},{9,1},{17,25},{25,17},{2,10},{10... | collective-permute-start | bytes 786440 | tf_op jit(solution)/shard_map/ppermute | solution.py:46
  27.4 0.0 copy-done.3
  27.4 0.9 shard_map.51
  28.3 0.1 shard_map.52.refs_8_
  28.4 0.0 collective-permute-done.8.refs_4_
  28.4 0.0 collective-permute-done.9.refs_5_
  28.4 0.0 collective-permute-done.10.refs_6_
  28.5 0.1 collective-permute-done.11.refs_7_
  28.6 0.0 copy-done.1
  28.6 2.7 %shard_map.53 = bf16[32,2,64,896]{3,2,1,0:T(8,128)(2,1)S(1)} custom-call(bf16[2,2048,896]{2,1,0:T(8,128)(2,1)S(1)} %copy-done.1, bf16[4,2,8,2048]{3,2,1,0:T(8,128)(2,1)S(1)} %pad_maximum_fusion.1.refs_0_, bf16[4,2,8,2048]{3,2,1,0:T(8,128)(2,1)S(1)} %shard_map.48.refs_1_, bf16[4,2,8,2048]{3,2,1,0:T(8,128)(2,1)S(1)} %shard_map.49.refs_2_, ...), custom_call_target="tpu_custom_call" | custom-call | flops 1879048192 | bytes 14680064 | tf_op jit(solution)/shard_map/pallas_call | solution.py:238
  31.2 87.1 %all_to_all.5.in_ref = bf16[32,2,64,896]{3,2,1,0:T(8,128)(2,1)S(1)} all-to-all(bf16[32,2,64,896]{3,2,1,0:T(8,128)(2,1)S(1)} %shard_map.53), channel_id=1, replica_groups={{0,4,8,12,2,6,10,14,16,20,24,28,18,22,26,30,1,5,9,13,3,7,11,15,17,21,25..., dimensions={0} | all-to-all | bytes 14680064 | tf_op jit(solution)/shard_map/all_to_all | solution.py:30
  118.4 3.1 %shard_map.54 = bf16[2,64,28672]{2,1,0:T(8,128)(2,1)} custom-call(bf16[32,2,64,896]{3,2,1,0:T(8,128)(2,1)S(1)} %all_to_all.5.in_ref), custom_call_target="tpu_custom_call" | custom-call | bytes 14680064 | tf_op jit(solution)/shard_map/pallas_call | solution.py:278
  (6 shorter events, 0.0 us)
Async XLA Ops:
  0.0 27.4 %copy-start.3 = (f32[16]{0:T(128)S(1)}, f32[16]{0:T(128)}, u32[]{:S(2)}) copy-start(f32[16]{0:T(128)} %weight_ref.1) | copy-start | bytes 196
  0.0 9.2 %collective-permute-start.4 = (bf16[1,2,8,8,896]{4,3,2,1,0:T(8,128)(2,1)}, bf16[1,2,8,8,896]{4,3,2,1,0:T(8,128)(2,1)S(1)}, u32[]{:S(2)}, u32[]{:S(2)}) collective-permute-start(bf16[1,2,8,8,896]{4,3,2,1,0:T(8,128)(2,1)} %bitcast.6), channel_id=1, source_target_pairs={{0,32},{8,104},{16,48},{24,120},{1,33},{9,105},{17,49},{25,121},{2... | collective-permute-start | bytes 688136 | tf_op jit(solution)/shard_map/ppermute | solution.py:68
  3.3 7.0 %collective-permute-start.2 = (bf16[1,2,8,2048]{3,2,1,0:T(8,128)(2,1)}, bf16[1,2,8,2048]{3,2,1,0:T(8,128)(2,1)S(1)}, u32[]{:S(2)}, u32[]{:S(2)}) collective-permute-start(bf16[1,2,8,2048]{3,2,1,0:T(8,128)(2,1)} %bitcast.2), channel_id=1, source_target_pairs={{0,16},{8,10},{16,1},{24,26},{1,17},{9,11},{17,0},{25,27},{2,18},{... | collective-permute-start | bytes 196616 | tf_op jit(solution)/shard_map/ppermute | solution.py:46
  4.6 5.7 %collective-permute-start.1 = (bf16[1,2,8,2048]{3,2,1,0:T(8,128)(2,1)}, bf16[1,2,8,2048]{3,2,1,0:T(8,128)(2,1)S(1)}, u32[]{:S(2)}, u32[]{:S(2)}) collective-permute-start(bf16[1,2,8,2048]{3,2,1,0:T(8,128)(2,1)} %bitcast.3), channel_id=1, source_target_pairs={{0,1},{8,12},{16,17},{24,28},{1,0},{9,13},{17,16},{25,29},{2,3},{1... | collective-permute-start | bytes 196616 | tf_op jit(solution)/shard_map/ppermute | solution.py:46
  7.2 3.6 %collective-permute-start = (bf16[1,2,8,2048]{3,2,1,0:T(8,128)(2,1)}, bf16[1,2,8,2048]{3,2,1,0:T(8,128)(2,1)S(1)}, u32[]{:S(2)}, u32[]{:S(2)}) collective-permute-start(bf16[1,2,8,2048]{3,2,1,0:T(8,128)(2,1)} %bitcast.4), channel_id=1, source_target_pairs={{0,17},{8,14},{16,0},{24,30},{1,16},{9,15},{17,1},{25,31},{2,19},{... | collective-permute-start | bytes 196616 | tf_op jit(solution)/shard_map/ppermute | solution.py:46
  8.3 0.9 copy-start.2
  10.2 11.2 %collective-permute-start.5 = (bf16[2,2,8,8,896]{4,3,2,1,0:T(8,128)(2,1)S(1)}, bf16[2,2,8,8,896]{4,3,2,1,0:T(8,128)(2,1)S(1)}, u32[]{:S(2)}, u32[]{:S(2)}) collective-permute-start(bf16[2,2,8,8,896]{4,3,2,1,0:T(8,128)(2,1)S(1)} %pad_maximum_fusion.near_ref), channel_id=1, source_target_pairs={{0,96},{8,40},{16,112},{24,56},{1,97},{9,41},{17,113},{25,57},{2,9... | collective-permute-start | bytes 1376264 | tf_op jit(solution)/shard_map/ppermute | solution.py:68
  10.9 10.5 %collective-permute-start.3 = (bf16[4,2,8,2048]{3,2,1,0:T(8,128)(2,1)S(1)}, bf16[4,2,8,2048]{3,2,1,0:T(8,128)(2,1)S(1)}, u32[]{:S(2)}, u32[]{:S(2)}) collective-permute-start(bf16[4,2,8,2048]{3,2,1,0:T(8,128)(2,1)S(1)} %pad_maximum_fusion.1.refs_0_), channel_id=1, source_target_pairs={{0,6},{8,25},{16,22},{24,8},{1,7},{9,24},{17,23},{25,9},{2,0},{10,... | collective-permute-start | bytes 786440 | tf_op jit(solution)/shard_map/ppermute | solution.py:46
  14.6 8.8 %collective-permute-start.6 = (bf16[4,2,8,2048]{3,2,1,0:T(8,128)(2,1)S(1)}, bf16[4,2,8,2048]{3,2,1,0:T(8,128)(2,1)S(1)}, u32[]{:S(2)}, u32[]{:S(2)}) collective-permute-start(bf16[4,2,8,2048]{3,2,1,0:T(8,128)(2,1)S(1)} %pad_maximum_fusion.1.refs_0_), channel_id=1, source_target_pairs={{0,4},{8,9},{16,20},{24,25},{1,5},{9,8},{17,21},{25,24},{2,6},{10,... | collective-permute-start | bytes 786440 | tf_op jit(solution)/shard_map/ppermute | solution.py:46
  14.6 10.1 %collective-permute-start.7 = (bf16[4,2,8,2048]{3,2,1,0:T(8,128)(2,1)S(1)}, bf16[4,2,8,2048]{3,2,1,0:T(8,128)(2,1)S(1)}, u32[]{:S(2)}, u32[]{:S(2)}) collective-permute-start(bf16[4,2,8,2048]{3,2,1,0:T(8,128)(2,1)S(1)} %pad_maximum_fusion.1.refs_0_), channel_id=1, source_target_pairs={{0,2},{8,24},{16,18},{24,9},{1,3},{9,25},{17,19},{25,8},{2,4},{10,... | collective-permute-start | bytes 786440 | tf_op jit(solution)/shard_map/ppermute | solution.py:46
  15.3 3.1 %copy-start = (bf16[2,2048,896]{2,1,0:T(8,128)(2,1)S(1)}, bf16[2,2048,896]{2,1,0:T(8,128)(2,1)}, u32[]{:S(2)}) copy-start(bf16[2,2048,896]{2,1,0:T(8,128)(2,1)} %base_ref.3) | copy-start | bytes 22020100
  18.4 10.2 %copy-start.1 = (bf16[2,2048,896]{2,1,0:T(8,128)(2,1)S(1)}, bf16[2,2048,896]{2,1,0:T(8,128)(2,1)}, u32[]{:S(2)}) copy-start(bf16[2,2048,896]{2,1,0:T(8,128)(2,1)} %base_ref.3) | copy-start | bytes 22020100
  18.4 10.0 %collective-permute-start.8 = (bf16[4,2,8,2048]{3,2,1,0:T(8,128)(2,1)S(1)}, bf16[4,2,8,2048]{3,2,1,0:T(8,128)(2,1)S(1)}, u32[]{:S(2)}, u32[]{:S(2)}) collective-permute-start(bf16[4,2,8,2048]{3,2,1,0:T(8,128)(2,1)S(1)} %pad_maximum_fusion.1.refs_0_), channel_id=1, source_target_pairs={{0,8},{8,0},{16,24},{24,16},{1,9},{9,1},{17,25},{25,17},{2,10},{10... | collective-permute-start | bytes 786440 | tf_op jit(solution)/shard_map/ppermute | solution.py:46
  21.4 7.0 %collective-permute-start.9 = (bf16[4,2,8,2048]{3,2,1,0:T(8,128)(2,1)S(1)}, bf16[4,2,8,2048]{3,2,1,0:T(8,128)(2,1)S(1)}, u32[]{:S(2)}, u32[]{:S(2)}) collective-permute-start(bf16[4,2,8,2048]{3,2,1,0:T(8,128)(2,1)S(1)} %shard_map.48.refs_1_), channel_id=1, source_target_pairs={{0,8},{8,0},{16,24},{24,16},{1,9},{9,1},{17,25},{25,17},{2,10},{10... | collective-permute-start | bytes 786440 | tf_op jit(solution)/shard_map/ppermute | solution.py:46
  23.4 5.0 %collective-permute-start.10 = (bf16[4,2,8,2048]{3,2,1,0:T(8,128)(2,1)S(1)}, bf16[4,2,8,2048]{3,2,1,0:T(8,128)(2,1)S(1)}, u32[]{:S(2)}, u32[]{:S(2)}) collective-permute-start(bf16[4,2,8,2048]{3,2,1,0:T(8,128)(2,1)S(1)} %shard_map.49.refs_2_), channel_id=1, source_target_pairs={{0,8},{8,0},{16,24},{24,16},{1,9},{9,1},{17,25},{25,17},{2,10},{10... | collective-permute-start | bytes 786440 | tf_op jit(solution)/shard_map/ppermute | solution.py:46
  24.7 3.9 %collective-permute-start.11 = (bf16[4,2,8,2048]{3,2,1,0:T(8,128)(2,1)S(1)}, bf16[4,2,8,2048]{3,2,1,0:T(8,128)(2,1)S(1)}, u32[]{:S(2)}, u32[]{:S(2)}) collective-permute-start(bf16[4,2,8,2048]{3,2,1,0:T(8,128)(2,1)S(1)} %shard_map.50.refs_3_), channel_id=1, source_target_pairs={{0,8},{8,0},{16,24},{24,16},{1,9},{9,1},{17,25},{25,17},{2,10},{10... | collective-permute-start | bytes 786440 | tf_op jit(solution)/shard_map/ppermute | solution.py:46

commit v5 on v4

--- a/solution.py
+++ b/solution.py
@@ -80,7 +80,7 @@
     near_sorted, scale = sort_near(participant_weight, near_up)
     b_sorted = sort_far(far_up, near_sorted)
     touched = touch(base, [])
-    others = [gate([piece], [touched, far_up])[0] for piece in others]
+    others = [gate([piece], [touched, b_sorted])[0] for piece in others]
     own = [mine, *others]
     other = [shift(piece, dcore=1) for piece in own]
     return own + other, b_sorted, scale
@@ -211,18 +211,18 @@
     ranks = BLOCKS * 8
     scale = scale_ref[...].reshape(ranks, 128)
     scale = jnp.concatenate([scale] * (tall // 128), axis=1)
-    for layer in range(layers):
-        right = b_ref[layer].reshape(ranks, cols)
-
-        @pl.loop(0, rows // tall, unroll=8)
-        def _(i):
-            span = pl.ds(pl.multiple_of(i * tall, tall), tall)
+    rights = [b_ref[layer].reshape(ranks, cols) for layer in range(layers)]
+
+    @pl.loop(0, rows // tall, unroll=8)
+    def _(i):
+        span = pl.ds(pl.multiple_of(i * tall, tall), tall)
+        for layer in range(layers):
             left = jnp.concatenate(
                 [ref[:, layer, :, span].reshape(-1, tall) for ref in a_refs]
             )
             left = (scale * left.astype(jnp.float32)).astype(jnp.bfloat16)
             delta = lax.dot_general(
-                left, right, (((0,), (0,)), ((), ())), preferred_element_type=jnp.float32
+                left, rights[layer], (((0,), (0,)), ((), ())), preferred_element_type=jnp.float32
             )
             merged = (base_ref[layer, span].astype(jnp.float32) + delta).astype(jnp.bfloat16)
             for part in range(per):

time: 122 us -> 122 us (level)
  no operation moved by 1% of the time
where the time goes in v5:
time: 122 us; the launch traced here: 121 us
  blocking collectives  87.1 us (71%)
  starting transfers between devices  20.7 us (17%)
  Pallas kernels  6.8 us (6%)
  local copies, waits for them, and re-layouts  3.96 us (3%)
  waiting for transfers between devices  1.74 us (1%)
    all_to_all x1, blocking collectives, exchange(): lax.all_to_all(pieces, TILE_AXES, split_axis=0, concat_axis=0, axis_index...  87.1 us
    ppermute x10, starting transfers between devices, shift(): return lax.ppermute(piece, ALL_AXES, pairs)  17.3 us
    unnamed x8, local copies, waits for them, and re-layouts  3.96 us
    ppermute x2, starting transfers between devices, trade(): return lax.ppermute(piece, ALL_AXES, pairs)  3.39 us
    pallas_call x1, Pallas kernels, settle(): pl.pallas_call(settle_kernel, in_specs=[pl.BlockSpec(memory_space=pltpu.V...  3.12 us
    pallas_call x1, Pallas kernels, merge(): pl.pallas_call(merge_kernel, in_specs=[vmem] * (len(a_pieces) + 3), out_s...  2.65 us
  transfers between devices with their start and end apart: 12, of which 2 were waited for; matrix products, arithmetic and copies ran while one was open for 1% of the time, Pallas kernels for 1%

profile of v5, /device:TPU:1, one launch (start us, length us, event | category | flops | bytes accessed | tf_op | source)
XLA Modules:
  0.0 121.5 jit_solution(13213092859993399855)
XLA Ops:
  0.0 0.0 copy-start.3
  0.0 3.3 %collective-permute-start.4 = (bf16[1,2,8,8,896]{4,3,2,1,0:T(8,128)(2,1)}, bf16[1,2,8,8,896]{4,3,2,1,0:T(8,128)(2,1)S(1)}, u32[]{:S(2)}, u32[]{:S(2)}) collective-permute-start(bf16[1,2,8,8,896]{4,3,2,1,0:T(8,128)(2,1)} %bitcast.6), channel_id=1, source_target_pairs={{0,32},{8,104},{16,48},{24,120},{1,33},{9,105},{17,49},{25,121},{2... | collective-permute-start | bytes 688136 | tf_op jit(solution)/shard_map/ppermute | solution.py:68
  3.3 1.3 %collective-permute-start.2 = (bf16[1,2,8,2048]{3,2,1,0:T(8,128)(2,1)}, bf16[1,2,8,2048]{3,2,1,0:T(8,128)(2,1)S(1)}, u32[]{:S(2)}, u32[]{:S(2)}) collective-permute-start(bf16[1,2,8,2048]{3,2,1,0:T(8,128)(2,1)} %bitcast.2), channel_id=1, source_target_pairs={{0,16},{8,10},{16,1},{24,26},{1,17},{9,11},{17,0},{25,27},{2,18},{... | collective-permute-start | bytes 196616 | tf_op jit(solution)/shard_map/ppermute | solution.py:46
  4.6 2.6 %collective-permute-start.1 = (bf16[1,2,8,2048]{3,2,1,0:T(8,128)(2,1)}, bf16[1,2,8,2048]{3,2,1,0:T(8,128)(2,1)S(1)}, u32[]{:S(2)}, u32[]{:S(2)}) collective-permute-start(bf16[1,2,8,2048]{3,2,1,0:T(8,128)(2,1)} %bitcast.3), channel_id=1, source_target_pairs={{0,1},{8,12},{16,17},{24,28},{1,0},{9,13},{17,16},{25,29},{2,3},{1... | collective-permute-start | bytes 196616 | tf_op jit(solution)/shard_map/ppermute | solution.py:46
  7.2 1.1 collective-permute-start
  8.3 0.0 copy-start.2
  8.3 0.9 copy-done.2
  9.2 0.0 collective-permute-done.4
  9.2 1.0 pad_maximum_fusion.near_ref
  10.2 0.1 collective-permute-start.5
  10.3 0.0 collective-permute-done.2
  10.3 0.0 collective-permute-done.1
  10.3 0.6 collective-permute-done
  10.9 3.7 %collective-permute-start.3 = (bf16[4,2,8,2048]{3,2,1,0:T(8,128)(2,1)S(1)}, bf16[4,2,8,2048]{3,2,1,0:T(8,128)(2,1)S(1)}, u32[]{:S(2)}, u32[]{:S(2)}) collective-permute-start(bf16[4,2,8,2048]{3,2,1,0:T(8,128)(2,1)S(1)} %pad_maximum_fusion.1.refs_0_), channel_id=1, source_target_pairs={{0,6},{8,25},{16,22},{24,8},{1,7},{9,24},{17,23},{25,9},{2,0},{10,... | collective-permute-start | bytes 786440 | tf_op jit(solution)/shard_map/ppermute | solution.py:46
  14.6 0.0 collective-permute-start.6
  14.6 0.7 collective-permute-start.7
  15.3 0.0 copy-start
  15.3 3.1 %copy-done = bf16[2,2048,896]{2,1,0:T(8,128)(2,1)S(1)} copy-done((bf16[2,2048,896]{2,1,0:T(8,128)(2,1)S(1)}, bf16[2,2048,896]{2,1,0:T(8,128)(2,1)}, u32[]{:S(2)}) %copy-start) | copy-done | bytes 7340056
  18.4 0.0 copy-start.1
  18.4 3.0 %collective-permute-start.8 = (bf16[4,2,8,2048]{3,2,1,0:T(8,128)(2,1)S(1)}, bf16[4,2,8,2048]{3,2,1,0:T(8,128)(2,1)S(1)}, u32[]{:S(2)}, u32[]{:S(2)}) collective-permute-start(bf16[4,2,8,2048]{3,2,1,0:T(8,128)(2,1)S(1)} %pad_maximum_fusion.1.refs_0_), channel_id=1, source_target_pairs={{0,8},{8,0},{16,24},{24,16},{1,9},{9,1},{17,25},{25,17},{2,10},{10... | collective-permute-start | bytes 786440 | tf_op jit(solution)/shard_map/ppermute | solution.py:46
  21.4 0.0 copy-done.3
  21.4 0.9 shard_map.48
  22.3 0.0 collective-permute-done.5.far_ref
  22.3 0.1 shard_map.49.refs_2_.refs_8_
  22.4 0.0 collective-permute-done.3.refs_0_
  22.5 0.9 collective-permute-start.9
  23.4 0.0 collective-permute-done.6.refs_0_
  23.4 1.3 %collective-permute-start.10 = (bf16[4,2,8,2048]{3,2,1,0:T(8,128)(2,1)S(1)}, bf16[4,2,8,2048]{3,2,1,0:T(8,128)(2,1)S(1)}, u32[]{:S(2)}, u32[]{:S(2)}) collective-permute-start(bf16[4,2,8,2048]{3,2,1,0:T(8,128)(2,1)S(1)} %shard_map.51.refs_2_), channel_id=1, source_target_pairs={{0,8},{8,0},{16,24},{24,16},{1,9},{9,1},{17,25},{25,17},{2,10},{10... | collective-permute-start | bytes 786440 | tf_op jit(solution)/shard_map/ppermute | solution.py:46
  24.7 0.0 collective-permute-done.7.refs_0_
  24.7 2.7 %collective-permute-start.11 = (bf16[4,2,8,2048]{3,2,1,0:T(8,128)(2,1)S(1)}, bf16[4,2,8,2048]{3,2,1,0:T(8,128)(2,1)S(1)}, u32[]{:S(2)}, u32[]{:S(2)}) collective-permute-start(bf16[4,2,8,2048]{3,2,1,0:T(8,128)(2,1)S(1)} %shard_map.52.refs_3_), channel_id=1, source_target_pairs={{0,8},{8,0},{16,24},{24,16},{1,9},{9,1},{17,25},{25,17},{2,10},{10... | collective-permute-start | bytes 786440 | tf_op jit(solution)/shard_map/ppermute | solution.py:46
  27.4 0.0 collective-permute-done.8.refs_4_
  27.4 0.0 collective-permute-done.9.refs_5_
  27.4 0.0 collective-permute-done.10.refs_6_
  27.4 1.1 collective-permute-done.11.refs_7_
  28.6 0.0 copy-done.1
  28.6 2.7 %shard_map.53 = bf16[32,2,64,896]{3,2,1,0:T(8,128)(2,1)S(1)} custom-call(bf16[2,2048,896]{2,1,0:T(8,128)(2,1)S(1)} %copy-done.1, bf16[4,2,8,2048]{3,2,1,0:T(8,128)(2,1)S(1)} %pad_maximum_fusion.1.refs_0_, bf16[4,2,8,2048]{3,2,1,0:T(8,128)(2,1)S(1)} %shard_map.50.refs_1_, bf16[4,2,8,2048]{3,2,1,0:T(8,128)(2,1)S(1)} %shard_map.51.refs_2_, ...), custom_call_target="tpu_custom_call" | custom-call | flops 1879048192 | bytes 14680064 | tf_op jit(solution)/shard_map/pallas_call | solution.py:238
  31.2 87.1 %all_to_all.5.in_ref = bf16[32,2,64,896]{3,2,1,0:T(8,128)(2,1)S(1)} all-to-all(bf16[32,2,64,896]{3,2,1,0:T(8,128)(2,1)S(1)} %shard_map.53), channel_id=1, replica_groups={{0,4,8,12,2,6,10,14,16,20,24,28,18,22,26,30,1,5,9,13,3,7,11,15,17,21,25..., dimensions={0} | all-to-all | bytes 14680064 | tf_op jit(solution)/shard_map/all_to_all | solution.py:30
  118.3 3.1 %shard_map.54 = bf16[2,64,28672]{2,1,0:T(8,128)(2,1)} custom-call(bf16[32,2,64,896]{3,2,1,0:T(8,128)(2,1)S(1)} %all_to_all.5.in_ref), custom_call_target="tpu_custom_call" | custom-call | bytes 14680064 | tf_op jit(solution)/shard_map/pallas_call | solution.py:278
  (6 shorter events, 0.0 us)
Async XLA Ops:
  0.0 21.4 %copy-start.3 = (f32[16]{0:T(128)S(1)}, f32[16]{0:T(128)}, u32[]{:S(2)}) copy-start(f32[16]{0:T(128)} %weight_ref.1) | copy-start | bytes 196
  0.0 9.2 %collective-permute-start.4 = (bf16[1,2,8,8,896]{4,3,2,1,0:T(8,128)(2,1)}, bf16[1,2,8,8,896]{4,3,2,1,0:T(8,128)(2,1)S(1)}, u32[]{:S(2)}, u32[]{:S(2)}) collective-permute-start(bf16[1,2,8,8,896]{4,3,2,1,0:T(8,128)(2,1)} %bitcast.6), channel_id=1, source_target_pairs={{0,32},{8,104},{16,48},{24,120},{1,33},{9,105},{17,49},{25,121},{2... | collective-permute-start | bytes 688136 | tf_op jit(solution)/shard_map/ppermute | solution.py:68
  3.3 7.0 %collective-permute-start.2 = (bf16[1,2,8,2048]{3,2,1,0:T(8,128)(2,1)}, bf16[1,2,8,2048]{3,2,1,0:T(8,128)(2,1)S(1)}, u32[]{:S(2)}, u32[]{:S(2)}) collective-permute-start(bf16[1,2,8,2048]{3,2,1,0:T(8,128)(2,1)} %bitcast.2), channel_id=1, source_target_pairs={{0,16},{8,10},{16,1},{24,26},{1,17},{9,11},{17,0},{25,27},{2,18},{... | collective-permute-start | bytes 196616 | tf_op jit(solution)/shard_map/ppermute | solution.py:46
  4.6 5.7 %collective-permute-start.1 = (bf16[1,2,8,2048]{3,2,1,0:T(8,128)(2,1)}, bf16[1,2,8,2048]{3,2,1,0:T(8,128)(2,1)S(1)}, u32[]{:S(2)}, u32[]{:S(2)}) collective-permute-start(bf16[1,2,8,2048]{3,2,1,0:T(8,128)(2,1)} %bitcast.3), channel_id=1, source_target_pairs={{0,1},{8,12},{16,17},{24,28},{1,0},{9,13},{17,16},{25,29},{2,3},{1... | collective-permute-start | bytes 196616 | tf_op jit(solution)/shard_map/ppermute | solution.py:46
  7.2 3.6 %collective-permute-start = (bf16[1,2,8,2048]{3,2,1,0:T(8,128)(2,1)}, bf16[1,2,8,2048]{3,2,1,0:T(8,128)(2,1)S(1)}, u32[]{:S(2)}, u32[]{:S(2)}) collective-permute-start(bf16[1,2,8,2048]{3,2,1,0:T(8,128)(2,1)} %bitcast.4), channel_id=1, source_target_pairs={{0,17},{8,14},{16,0},{24,30},{1,16},{9,15},{17,1},{25,31},{2,19},{... | collective-permute-start | bytes 196616 | tf_op jit(solution)/shard_map/ppermute | solution.py:46
  8.3 0.9 copy-start.2
  10.2 12.1 %collective-permute-start.5 = (bf16[2,2,8,8,896]{4,3,2,1,0:T(8,128)(2,1)S(1)}, bf16[2,2,8,8,896]{4,3,2,1,0:T(8,128)(2,1)S(1)}, u32[]{:S(2)}, u32[]{:S(2)}) collective-permute-start(bf16[2,2,8,8,896]{4,3,2,1,0:T(8,128)(2,1)S(1)} %pad_maximum_fusion.near_ref), channel_id=1, source_target_pairs={{0,96},{8,40},{16,112},{24,56},{1,97},{9,41},{17,113},{25,57},{2,9... | collective-permute-start | bytes 1376264 | tf_op jit(solution)/shard_map/ppermute | solution.py:68
  10.9 11.5 %collective-permute-start.3 = (bf16[4,2,8,2048]{3,2,1,0:T(8,128)(2,1)S(1)}, bf16[4,2,8,2048]{3,2,1,0:T(8,128)(2,1)S(1)}, u32[]{:S(2)}, u32[]{:S(2)}) collective-permute-start(bf16[4,2,8,2048]{3,2,1,0:T(8,128)(2,1)S(1)} %pad_maximum_fusion.1.refs_0_), channel_id=1, source_target_pairs={{0,6},{8,25},{16,22},{24,8},{1,7},{9,24},{17,23},{25,9},{2,0},{10,... | collective-permute-start | bytes 786440 | tf_op jit(solution)/shard_map/ppermute | solution.py:46
  14.6 8.8 %collective-permute-start.6 = (bf16[4,2,8,2048]{3,2,1,0:T(8,128)(2,1)S(1)}, bf16[4,2,8,2048]{3,2,1,0:T(8,128)(2,1)S(1)}, u32[]{:S(2)}, u32[]{:S(2)}) collective-permute-start(bf16[4,2,8,2048]{3,2,1,0:T(8,128)(2,1)S(1)} %pad_maximum_fusion.1.refs_0_), channel_id=1, source_target_pairs={{0,4},{8,9},{16,20},{24,25},{1,5},{9,8},{17,21},{25,24},{2,6},{10,... | collective-permute-start | bytes 786440 | tf_op jit(solution)/shard_map/ppermute | solution.py:46
  14.6 10.1 %collective-permute-start.7 = (bf16[4,2,8,2048]{3,2,1,0:T(8,128)(2,1)S(1)}, bf16[4,2,8,2048]{3,2,1,0:T(8,128)(2,1)S(1)}, u32[]{:S(2)}, u32[]{:S(2)}) collective-permute-start(bf16[4,2,8,2048]{3,2,1,0:T(8,128)(2,1)S(1)} %pad_maximum_fusion.1.refs_0_), channel_id=1, source_target_pairs={{0,2},{8,24},{16,18},{24,9},{1,3},{9,25},{17,19},{25,8},{2,4},{10,... | collective-permute-start | bytes 786440 | tf_op jit(solution)/shard_map/ppermute | solution.py:46
  15.3 3.1 %copy-start = (bf16[2,2048,896]{2,1,0:T(8,128)(2,1)S(1)}, bf16[2,2048,896]{2,1,0:T(8,128)(2,1)}, u32[]{:S(2)}) copy-start(bf16[2,2048,896]{2,1,0:T(8,128)(2,1)} %base_ref.3) | copy-start | bytes 22020100
  18.4 10.2 %copy-start.1 = (bf16[2,2048,896]{2,1,0:T(8,128)(2,1)S(1)}, bf16[2,2048,896]{2,1,0:T(8,128)(2,1)}, u32[]{:S(2)}) copy-start(bf16[2,2048,896]{2,1,0:T(8,128)(2,1)} %base_ref.3) | copy-start | bytes 22020100
  18.4 9.0 %collective-permute-start.8 = (bf16[4,2,8,2048]{3,2,1,0:T(8,128)(2,1)S(1)}, bf16[4,2,8,2048]{3,2,1,0:T(8,128)(2,1)S(1)}, u32[]{:S(2)}, u32[]{:S(2)}) collective-permute-start(bf16[4,2,8,2048]{3,2,1,0:T(8,128)(2,1)S(1)} %pad_maximum_fusion.1.refs_0_), channel_id=1, source_target_pairs={{0,8},{8,0},{16,24},{24,16},{1,9},{9,1},{17,25},{25,17},{2,10},{10... | collective-permute-start | bytes 786440 | tf_op jit(solution)/shard_map/ppermute | solution.py:46
  22.5 4.9 %collective-permute-start.9 = (bf16[4,2,8,2048]{3,2,1,0:T(8,128)(2,1)S(1)}, bf16[4,2,8,2048]{3,2,1,0:T(8,128)(2,1)S(1)}, u32[]{:S(2)}, u32[]{:S(2)}) collective-permute-start(bf16[4,2,8,2048]{3,2,1,0:T(8,128)(2,1)S(1)} %shard_map.50.refs_1_), channel_id=1, source_target_pairs={{0,8},{8,0},{16,24},{24,16},{1,9},{9,1},{17,25},{25,17},{2,10},{10... | collective-permute-start | bytes 786440 | tf_op jit(solution)/shard_map/ppermute | solution.py:46
  23.4 4.0 %collective-permute-start.10 = (bf16[4,2,8,2048]{3,2,1,0:T(8,128)(2,1)S(1)}, bf16[4,2,8,2048]{3,2,1,0:T(8,128)(2,1)S(1)}, u32[]{:S(2)}, u32[]{:S(2)}) collective-permute-start(bf16[4,2,8,2048]{3,2,1,0:T(8,128)(2,1)S(1)} %shard_map.51.refs_2_), channel_id=1, source_target_pairs={{0,8},{8,0},{16,24},{24,16},{1,9},{9,1},{17,25},{25,17},{2,10},{10... | collective-permute-start | bytes 786440 | tf_op jit(solution)/shard_map/ppermute | solution.py:46
  24.7 3.9 %collective-permute-start.11 = (bf16[4,2,8,2048]{3,2,1,0:T(8,128)(2,1)S(1)}, bf16[4,2,8,2048]{3,2,1,0:T(8,128)(2,1)S(1)}, u32[]{:S(2)}, u32[]{:S(2)}) collective-permute-start(bf16[4,2,8,2048]{3,2,1,0:T(8,128)(2,1)S(1)} %shard_map.52.refs_3_), channel_id=1, source_target_pairs={{0,8},{8,0},{16,24},{24,16},{1,9},{9,1},{17,25},{25,17},{2,10},{10... | collective-permute-start | bytes 786440 | tf_op jit(solution)/shard_map/ppermute | solution.py:46

commit v6 on v5

--- a/solution.py
+++ b/solution.py
@@ -18,7 +18,7 @@
 
 
 def spot_of(y, z, core):
-    return z * 8 + (y % 2) * 4 + core * 2 + y // 2
+    return (z // 2) * 16 + core * 8 + (z % 2) * 4 + (y % 2) * 2 + y // 2
 
 
 def exchange(pieces):

time: 122 us -> 123 us (level)
  no operation moved by 1% of the time
where the time goes in v6:
time: 123 us
  blocking collectives  88.2 us (72%)
  starting transfers between devices  20.7 us (17%)
  Pallas kernels  6.8 us (6%)
  local copies, waits for them, and re-layouts  3.96 us (3%)
  waiting for transfers between devices  1.74 us (1%)
    all_to_all x1, blocking collectives, exchange(): lax.all_to_all(pieces, TILE_AXES, split_axis=0, concat_axis=0, axis_index...  88.2 us
    ppermute x10, starting transfers between devices, shift(): return lax.ppermute(piece, ALL_AXES, pairs)  17.3 us
    unnamed x8, local copies, waits for them, and re-layouts  3.96 us
    ppermute x2, starting transfers between devices, trade(): return lax.ppermute(piece, ALL_AXES, pairs)  3.39 us
    pallas_call x1, Pallas kernels, settle(): pl.pallas_call(settle_kernel, in_specs=[pl.BlockSpec(memory_space=pltpu.V...  3.12 us
    pallas_call x1, Pallas kernels, merge(): pl.pallas_call(merge_kernel, in_specs=[vmem] * (len(a_pieces) + 3), out_s...  2.65 us
  transfers between devices with their start and end apart: 12, of which 2 were waited for; matrix products, arithmetic and copies ran while one was open for 1% of the time, Pallas kernels for 1%

profile of v6, /device:TPU:1, one launch (start us, length us, event | category | flops | bytes accessed | tf_op | source)
XLA Modules:
  0.0 122.5 jit_solution(10741524004825899728)
XLA Ops:
  0.0 0.0 copy-start.3
  0.0 3.3 %collective-permute-start.4 = (bf16[1,2,8,8,896]{4,3,2,1,0:T(8,128)(2,1)}, bf16[1,2,8,8,896]{4,3,2,1,0:T(8,128)(2,1)S(1)}, u32[]{:S(2)}, u32[]{:S(2)}) collective-permute-start(bf16[1,2,8,8,896]{4,3,2,1,0:T(8,128)(2,1)} %bitcast.6), channel_id=1, source_target_pairs={{0,32},{8,104},{16,48},{24,120},{1,33},{9,105},{17,49},{25,121},{2... | collective-permute-start | bytes 688136 | tf_op jit(solution)/shard_map/ppermute | solution.py:68
  3.3 1.3 %collective-permute-start.2 = (bf16[1,2,8,2048]{3,2,1,0:T(8,128)(2,1)}, bf16[1,2,8,2048]{3,2,1,0:T(8,128)(2,1)S(1)}, u32[]{:S(2)}, u32[]{:S(2)}) collective-permute-start(bf16[1,2,8,2048]{3,2,1,0:T(8,128)(2,1)} %bitcast.2), channel_id=1, source_target_pairs={{0,16},{8,10},{16,1},{24,26},{1,17},{9,11},{17,0},{25,27},{2,18},{... | collective-permute-start | bytes 196616 | tf_op jit(solution)/shard_map/ppermute | solution.py:46
  4.6 2.6 %collective-permute-start.1 = (bf16[1,2,8,2048]{3,2,1,0:T(8,128)(2,1)}, bf16[1,2,8,2048]{3,2,1,0:T(8,128)(2,1)S(1)}, u32[]{:S(2)}, u32[]{:S(2)}) collective-permute-start(bf16[1,2,8,2048]{3,2,1,0:T(8,128)(2,1)} %bitcast.3), channel_id=1, source_target_pairs={{0,1},{8,12},{16,17},{24,28},{1,0},{9,13},{17,16},{25,29},{2,3},{1... | collective-permute-start | bytes 196616 | tf_op jit(solution)/shard_map/ppermute | solution.py:46
  7.2 1.1 collective-permute-start
  8.3 0.0 copy-start.2
  8.3 0.9 copy-done.2
  9.2 0.0 collective-permute-done.4
  9.2 1.0 pad_maximum_fusion.near_ref
  10.2 0.1 collective-permute-start.5
  10.3 0.0 collective-permute-done.2
  10.3 0.0 collective-permute-done.1
  10.3 0.6 collective-permute-done
  10.9 3.7 %collective-permute-start.3 = (bf16[4,2,8,2048]{3,2,1,0:T(8,128)(2,1)S(1)}, bf16[4,2,8,2048]{3,2,1,0:T(8,128)(2,1)S(1)}, u32[]{:S(2)}, u32[]{:S(2)}) collective-permute-start(bf16[4,2,8,2048]{3,2,1,0:T(8,128)(2,1)S(1)} %pad_maximum_fusion.1.refs_0_), channel_id=1, source_target_pairs={{0,6},{8,25},{16,22},{24,8},{1,7},{9,24},{17,23},{25,9},{2,0},{10,... | collective-permute-start | bytes 786440 | tf_op jit(solution)/shard_map/ppermute | solution.py:46
  14.6 0.0 collective-permute-start.6
  14.6 0.7 collective-permute-start.7
  15.3 0.0 copy-start
  15.3 3.1 %copy-done = bf16[2,2048,896]{2,1,0:T(8,128)(2,1)S(1)} copy-done((bf16[2,2048,896]{2,1,0:T(8,128)(2,1)S(1)}, bf16[2,2048,896]{2,1,0:T(8,128)(2,1)}, u32[]{:S(2)}) %copy-start) | copy-done | bytes 7340056
  18.4 0.0 copy-start.1
  18.4 3.0 %collective-permute-start.8 = (bf16[4,2,8,2048]{3,2,1,0:T(8,128)(2,1)S(1)}, bf16[4,2,8,2048]{3,2,1,0:T(8,128)(2,1)S(1)}, u32[]{:S(2)}, u32[]{:S(2)}) collective-permute-start(bf16[4,2,8,2048]{3,2,1,0:T(8,128)(2,1)S(1)} %pad_maximum_fusion.1.refs_0_), channel_id=1, source_target_pairs={{0,8},{8,0},{16,24},{24,16},{1,9},{9,1},{17,25},{25,17},{2,10},{10... | collective-permute-start | bytes 786440 | tf_op jit(solution)/shard_map/ppermute | solution.py:46
  21.4 0.0 copy-done.3
  21.4 0.9 shard_map.48
  22.3 0.0 collective-permute-done.5.far_ref
  22.3 0.1 shard_map.49.refs_2_.refs_8_
  22.4 0.0 collective-permute-done.3.refs_0_
  22.5 0.9 collective-permute-start.9
  23.4 0.0 collective-permute-done.6.refs_0_
  23.4 1.3 %collective-permute-start.10 = (bf16[4,2,8,2048]{3,2,1,0:T(8,128)(2,1)S(1)}, bf16[4,2,8,2048]{3,2,1,0:T(8,128)(2,1)S(1)}, u32[]{:S(2)}, u32[]{:S(2)}) collective-permute-start(bf16[4,2,8,2048]{3,2,1,0:T(8,128)(2,1)S(1)} %shard_map.51.refs_2_), channel_id=1, source_target_pairs={{0,8},{8,0},{16,24},{24,16},{1,9},{9,1},{17,25},{25,17},{2,10},{10... | collective-permute-start | bytes 786440 | tf_op jit(solution)/shard_map/ppermute | solution.py:46
  24.7 0.0 collective-permute-done.7.refs_0_
  24.7 2.7 %collective-permute-start.11 = (bf16[4,2,8,2048]{3,2,1,0:T(8,128)(2,1)S(1)}, bf16[4,2,8,2048]{3,2,1,0:T(8,128)(2,1)S(1)}, u32[]{:S(2)}, u32[]{:S(2)}) collective-permute-start(bf16[4,2,8,2048]{3,2,1,0:T(8,128)(2,1)S(1)} %shard_map.52.refs_3_), channel_id=1, source_target_pairs={{0,8},{8,0},{16,24},{24,16},{1,9},{9,1},{17,25},{25,17},{2,10},{10... | collective-permute-start | bytes 786440 | tf_op jit(solution)/shard_map/ppermute | solution.py:46
  27.4 0.0 collective-permute-done.8.refs_4_
  27.4 0.0 collective-permute-done.9.refs_5_
  27.4 0.0 collective-permute-done.10.refs_6_
  27.4 1.1 collective-permute-done.11.refs_7_
  28.6 0.0 copy-done.1
  28.6 2.7 %shard_map.53 = bf16[32,2,64,896]{3,2,1,0:T(8,128)(2,1)S(1)} custom-call(bf16[2,2048,896]{2,1,0:T(8,128)(2,1)S(1)} %copy-done.1, bf16[4,2,8,2048]{3,2,1,0:T(8,128)(2,1)S(1)} %pad_maximum_fusion.1.refs_0_, bf16[4,2,8,2048]{3,2,1,0:T(8,128)(2,1)S(1)} %shard_map.50.refs_1_, bf16[4,2,8,2048]{3,2,1,0:T(8,128)(2,1)S(1)} %shard_map.51.refs_2_, ...), custom_call_target="tpu_custom_call" | custom-call | flops 1879048192 | bytes 14680064 | tf_op jit(solution)/shard_map/pallas_call | solution.py:238
  31.2 88.2 %all_to_all.5.in_ref = bf16[32,2,64,896]{3,2,1,0:T(8,128)(2,1)S(1)} all-to-all(bf16[32,2,64,896]{3,2,1,0:T(8,128)(2,1)S(1)} %shard_map.53), channel_id=1, replica_groups={{0,4,2,6,16,20,18,22,8,12,10,14,24,28,26,30,1,5,3,7,17,21,19,23,9,13,11..., dimensions={0} | all-to-all | bytes 14680064 | tf_op jit(solution)/shard_map/all_to_all | solution.py:30
  119.4 3.1 %shard_map.54 = bf16[2,64,28672]{2,1,0:T(8,128)(2,1)} custom-call(bf16[32,2,64,896]{3,2,1,0:T(8,128)(2,1)S(1)} %all_to_all.5.in_ref), custom_call_target="tpu_custom_call" | custom-call | bytes 14680064 | tf_op jit(solution)/shard_map/pallas_call | solution.py:278
  (6 shorter events, 0.0 us)
Async XLA Ops:
  0.0 21.4 %copy-start.3 = (f32[16]{0:T(128)S(1)}, f32[16]{0:T(128)}, u32[]{:S(2)}) copy-start(f32[16]{0:T(128)} %weight_ref.1) | copy-start | bytes 196
  0.0 9.2 %collective-permute-start.4 = (bf16[1,2,8,8,896]{4,3,2,1,0:T(8,128)(2,1)}, bf16[1,2,8,8,896]{4,3,2,1,0:T(8,128)(2,1)S(1)}, u32[]{:S(2)}, u32[]{:S(2)}) collective-permute-start(bf16[1,2,8,8,896]{4,3,2,1,0:T(8,128)(2,1)} %bitcast.6), channel_id=1, source_target_pairs={{0,32},{8,104},{16,48},{24,120},{1,33},{9,105},{17,49},{25,121},{2... | collective-permute-start | bytes 688136 | tf_op jit(solution)/shard_map/ppermute | solution.py:68
  3.3 7.0 %collective-permute-start.2 = (bf16[1,2,8,2048]{3,2,1,0:T(8,128)(2,1)}, bf16[1,2,8,2048]{3,2,1,0:T(8,128)(2,1)S(1)}, u32[]{:S(2)}, u32[]{:S(2)}) collective-permute-start(bf16[1,2,8,2048]{3,2,1,0:T(8,128)(2,1)} %bitcast.2), channel_id=1, source_target_pairs={{0,16},{8,10},{16,1},{24,26},{1,17},{9,11},{17,0},{25,27},{2,18},{... | collective-permute-start | bytes 196616 | tf_op jit(solution)/shard_map/ppermute | solution.py:46
  4.6 5.7 %collective-permute-start.1 = (bf16[1,2,8,2048]{3,2,1,0:T(8,128)(2,1)}, bf16[1,2,8,2048]{3,2,1,0:T(8,128)(2,1)S(1)}, u32[]{:S(2)}, u32[]{:S(2)}) collective-permute-start(bf16[1,2,8,2048]{3,2,1,0:T(8,128)(2,1)} %bitcast.3), channel_id=1, source_target_pairs={{0,1},{8,12},{16,17},{24,28},{1,0},{9,13},{17,16},{25,29},{2,3},{1... | collective-permute-start | bytes 196616 | tf_op jit(solution)/shard_map/ppermute | solution.py:46
  7.2 3.6 %collective-permute-start = (bf16[1,2,8,2048]{3,2,1,0:T(8,128)(2,1)}, bf16[1,2,8,2048]{3,2,1,0:T(8,128)(2,1)S(1)}, u32[]{:S(2)}, u32[]{:S(2)}) collective-permute-start(bf16[1,2,8,2048]{3,2,1,0:T(8,128)(2,1)} %bitcast.4), channel_id=1, source_target_pairs={{0,17},{8,14},{16,0},{24,30},{1,16},{9,15},{17,1},{25,31},{2,19},{... | collective-permute-start | bytes 196616 | tf_op jit(solution)/shard_map/ppermute | solution.py:46
  8.3 0.9 copy-start.2
  10.2 12.1 %collective-permute-start.5 = (bf16[2,2,8,8,896]{4,3,2,1,0:T(8,128)(2,1)S(1)}, bf16[2,2,8,8,896]{4,3,2,1,0:T(8,128)(2,1)S(1)}, u32[]{:S(2)}, u32[]{:S(2)}) collective-permute-start(bf16[2,2,8,8,896]{4,3,2,1,0:T(8,128)(2,1)S(1)} %pad_maximum_fusion.near_ref), channel_id=1, source_target_pairs={{0,96},{8,40},{16,112},{24,56},{1,97},{9,41},{17,113},{25,57},{2,9... | collective-permute-start | bytes 1376264 | tf_op jit(solution)/shard_map/ppermute | solution.py:68
  10.9 11.5 %collective-permute-start.3 = (bf16[4,2,8,2048]{3,2,1,0:T(8,128)(2,1)S(1)}, bf16[4,2,8,2048]{3,2,1,0:T(8,128)(2,1)S(1)}, u32[]{:S(2)}, u32[]{:S(2)}) collective-permute-start(bf16[4,2,8,2048]{3,2,1,0:T(8,128)(2,1)S(1)} %pad_maximum_fusion.1.refs_0_), channel_id=1, source_target_pairs={{0,6},{8,25},{16,22},{24,8},{1,7},{9,24},{17,23},{25,9},{2,0},{10,... | collective-permute-start | bytes 786440 | tf_op jit(solution)/shard_map/ppermute | solution.py:46
  14.6 8.8 %collective-permute-start.6 = (bf16[4,2,8,2048]{3,2,1,0:T(8,128)(2,1)S(1)}, bf16[4,2,8,2048]{3,2,1,0:T(8,128)(2,1)S(1)}, u32[]{:S(2)}, u32[]{:S(2)}) collective-permute-start(bf16[4,2,8,2048]{3,2,1,0:T(8,128)(2,1)S(1)} %pad_maximum_fusion.1.refs_0_), channel_id=1, source_target_pairs={{0,4},{8,9},{16,20},{24,25},{1,5},{9,8},{17,21},{25,24},{2,6},{10,... | collective-permute-start | bytes 786440 | tf_op jit(solution)/shard_map/ppermute | solution.py:46
  14.6 10.1 %collective-permute-start.7 = (bf16[4,2,8,2048]{3,2,1,0:T(8,128)(2,1)S(1)}, bf16[4,2,8,2048]{3,2,1,0:T(8,128)(2,1)S(1)}, u32[]{:S(2)}, u32[]{:S(2)}) collective-permute-start(bf16[4,2,8,2048]{3,2,1,0:T(8,128)(2,1)S(1)} %pad_maximum_fusion.1.refs_0_), channel_id=1, source_target_pairs={{0,2},{8,24},{16,18},{24,9},{1,3},{9,25},{17,19},{25,8},{2,4},{10,... | collective-permute-start | bytes 786440 | tf_op jit(solution)/shard_map/ppermute | solution.py:46
  15.3 3.1 %copy-start = (bf16[2,2048,896]{2,1,0:T(8,128)(2,1)S(1)}, bf16[2,2048,896]{2,1,0:T(8,128)(2,1)}, u32[]{:S(2)}) copy-start(bf16[2,2048,896]{2,1,0:T(8,128)(2,1)} %base_ref.3) | copy-start | bytes 22020100
  18.4 10.2 %copy-start.1 = (bf16[2,2048,896]{2,1,0:T(8,128)(2,1)S(1)}, bf16[2,2048,896]{2,1,0:T(8,128)(2,1)}, u32[]{:S(2)}) copy-start(bf16[2,2048,896]{2,1,0:T(8,128)(2,1)} %base_ref.3) | copy-start | bytes 22020100
  18.4 9.0 %collective-permute-start.8 = (bf16[4,2,8,2048]{3,2,1,0:T(8,128)(2,1)S(1)}, bf16[4,2,8,2048]{3,2,1,0:T(8,128)(2,1)S(1)}, u32[]{:S(2)}, u32[]{:S(2)}) collective-permute-start(bf16[4,2,8,2048]{3,2,1,0:T(8,128)(2,1)S(1)} %pad_maximum_fusion.1.refs_0_), channel_id=1, source_target_pairs={{0,8},{8,0},{16,24},{24,16},{1,9},{9,1},{17,25},{25,17},{2,10},{10... | collective-permute-start | bytes 786440 | tf_op jit(solution)/shard_map/ppermute | solution.py:46
  22.5 4.9 %collective-permute-start.9 = (bf16[4,2,8,2048]{3,2,1,0:T(8,128)(2,1)S(1)}, bf16[4,2,8,2048]{3,2,1,0:T(8,128)(2,1)S(1)}, u32[]{:S(2)}, u32[]{:S(2)}) collective-permute-start(bf16[4,2,8,2048]{3,2,1,0:T(8,128)(2,1)S(1)} %shard_map.50.refs_1_), channel_id=1, source_target_pairs={{0,8},{8,0},{16,24},{24,16},{1,9},{9,1},{17,25},{25,17},{2,10},{10... | collective-permute-start | bytes 786440 | tf_op jit(solution)/shard_map/ppermute | solution.py:46
  23.4 4.0 %collective-permute-start.10 = (bf16[4,2,8,2048]{3,2,1,0:T(8,128)(2,1)S(1)}, bf16[4,2,8,2048]{3,2,1,0:T(8,128)(2,1)S(1)}, u32[]{:S(2)}, u32[]{:S(2)}) collective-permute-start(bf16[4,2,8,2048]{3,2,1,0:T(8,128)(2,1)S(1)} %shard_map.51.refs_2_), channel_id=1, source_target_pairs={{0,8},{8,0},{16,24},{24,16},{1,9},{9,1},{17,25},{25,17},{2,10},{10... | collective-permute-start | bytes 786440 | tf_op jit(solution)/shard_map/ppermute | solution.py:46
  24.7 3.9 %collective-permute-start.11 = (bf16[4,2,8,2048]{3,2,1,0:T(8,128)(2,1)S(1)}, bf16[4,2,8,2048]{3,2,1,0:T(8,128)(2,1)S(1)}, u32[]{:S(2)}, u32[]{:S(2)}) collective-permute-start(bf16[4,2,8,2048]{3,2,1,0:T(8,128)(2,1)S(1)} %shard_map.52.refs_3_), channel_id=1, source_target_pairs={{0,8},{8,0},{16,24},{24,16},{1,9},{9,1},{17,25},{25,17},{2,10},{10... | collective-permute-start | bytes 786440 | tf_op jit(solution)/shard_map/ppermute | solution.py:46
